TPU v7x, 32 devices: a whole 2x2x4 slice. The times are simulated.
32 devices in a mesh: ctx: 16 (over z, x, core), wsh: 2 (over y).
Axes of the slice: x: 2, y: 2, z: 4, core: 2. Of those that a mesh axis runs over, the one named last changes fastest.
Arguments:
- hidden_in: bfloat16 [2, 2, 8192, 768], P(None, 'wsh', 'ctx'), may hold values from -6 to 6
- segment_ids: int32 [2, 2, 8192], P(None, 'wsh'), may hold values from 0 to 10, never falling along the last dimension, each value on 1 to 1537 neighbouring positions
- out_grad: bfloat16 [2, 2, 8192, 768], P(None, 'wsh', 'ctx'), may hold values from -6 to 6
- query_w: bfloat16 [768, 384], P('wsh'), may hold values from -0.625 to 0.625
- query_b: bfloat16 [384], P('wsh'), may hold values from -3 to 3
- key_w: bfloat16 [768, 384], P('wsh'), may hold values from -0.21875 to 0.21875
- value_w: bfloat16 [768, 384], P('wsh'), may hold values from -0.21875 to 0.21875
- value_b: bfloat16 [384], P('wsh'), may hold values from -3 to 3
- depth_kernel: bfloat16 [9, 768], P(None, 'wsh'), may hold values from -2 to 2
- point_w: bfloat16 [768, 384], P('wsh'), may hold values from -0.21875 to 0.21875
- point_b: bfloat16 [384], P('wsh'), may hold values from -3 to 3
- kernel_w: bfloat16 [384, 54], P('wsh'), may hold values from -0.078125 to 0.078125
- kernel_b: bfloat16 [54], P('wsh'), may hold values from -3 to 3
- conv_w: bfloat16 [768, 384], P('wsh'), may hold values from -0.21875 to 0.21875
- conv_b: bfloat16 [384], P('wsh'), may hold values from -3 to 3
- output_w: bfloat16 [768, 768], P('wsh'), may hold values from -0.21875 to 0.21875
- output_b: bfloat16 [768], P('wsh'), may hold values from -3 to 3
- norm1_gain: bfloat16 [768], P('wsh'), may hold values from 0.5 to 1.5
- norm1_bias: bfloat16 [768], P('wsh'), may hold values from -3 to 3
- inner_w: bfloat16 [2, 384, 1536], P(None, 'wsh'), may hold values from -0.3125 to 0.3125
- inner_b: bfloat16 [3072], P('wsh'), may hold values from -3 to 3
- outer_w: bfloat16 [2, 1536, 384], P(None, 'wsh'), may hold values from -0.15625 to 0.15625
- outer_b: bfloat16 [768], P('wsh'), may hold values from -3 to 3
- norm2_gain: bfloat16 [768], P('wsh'), may hold values from 0.5 to 1.5
- norm2_bias: bfloat16 [768], P('wsh'), may hold values from -3 to 3
Outputs:
- output: bfloat16 [2, 2, 8192, 768], P(None, 'wsh', 'ctx')
- input_grad: float32 [2, 2, 8192, 768], P(None, 'wsh', 'ctx')
- grad_query_w: float32 [768, 384], P('wsh')
- grad_query_b: float32 [384], P('wsh')
- grad_key_w: float32 [768, 384], P('wsh')
- grad_value_w: float32 [768, 384], P('wsh')
- grad_value_b: float32 [384], P('wsh')
- grad_depth_kernel: float32 [9, 768], P(None, 'wsh')
- grad_point_w: float32 [768, 384], P('wsh')
- grad_point_b: float32 [384], P('wsh')
- grad_kernel_w: float32 [384, 54], P('wsh')
- grad_kernel_b: float32 [54], P('wsh')
- grad_conv_w: float32 [768, 384], P('wsh')
- grad_conv_b: float32 [384], P('wsh')
- grad_output_w: float32 [768, 768], P('wsh')
- grad_output_b: float32 [768], P('wsh')
- grad_norm1_gain: float32 [768], P('wsh')
- grad_norm1_bias: float32 [768], P('wsh')
- grad_inner_w: float32 [2, 384, 1536], P(None, 'wsh')
- grad_inner_b: float32 [3072], P('wsh')
- grad_outer_w: float32 [2, 1536, 384], P(None, 'wsh')
- grad_outer_b: float32 [768], P('wsh')
- grad_norm2_gain: float32 [768], P('wsh')
- grad_norm2_bias: float32 [768], P('wsh')
Inputs may be any that keep to these rules, and one draw needn't show every extreme that they name: `segment_ids`: within each sequence the document numbers never fall; each document has 1 to 1537 tokens, and one has exactly 1537.
All inputs are finite; a program needn't handle non-finite values.
Results may differ from a plain program's by a relative error of at most 0.015.
The roundings to bfloat16 on the way count: a program that leaves them out, or rounds other values in their place, can miss the bound.
Values may be sent and summed in bfloat16 or wider, within the bound.
A program may use at most 256 MiB of HBM per device.

v0:
```python
import jax
import jax.numpy as jnp
from jax import lax
from jax.sharding import PartitionSpec as P

HEADS = 6
HEAD_DIM = 64
KERNEL = 9
GROUPS = 2
HOPS = 2


def passed_along(shard, axis, by):
    count = lax.axis_size(axis)
    pairs = [(i, i + by) for i in range(count) if 0 <= i + by < count]
    return lax.ppermute(shard, axis, pairs)


def for_sending(shard):

    def short(part):
        return part.astype(jnp.bfloat16) if part.dtype == jnp.float32 else part

    return jax.tree.map(short, shard)


def with_halo(block, sides, width):
    for axis, dim in sides:
        count = lax.axis_size(axis)
        forward = [(i, i + 1) for i in range(count - 1)]
        backward = [(target, source) for source, target in forward]
        low = lax.ppermute(
            lax.slice_in_dim(block, block.shape[dim] - width, None, axis=dim), axis, forward
        )
        high = lax.ppermute(lax.slice_in_dim(block, 0, width, axis=dim), axis, backward)
        block = jnp.concatenate([low, block, high], axis=dim)
    return block


def layer_norm(values, gain, shift):
    center = values - jnp.mean(values, axis=-1, keepdims=True)
    spread = jnp.mean(center * center, axis=-1, keepdims=True)
    return center * lax.rsqrt(spread + 1e-05) * gain + shift


def gelu_exact(values):
    return jax.nn.gelu(values, approximate=False)


def kernel_softmax(values):
    return jax.nn.softmax(values, axis=-1)


def product(left, right):
    return jnp.dot(left, right, preferred_element_type=jnp.float32)


def product_tn(left, right):
    return jnp.einsum("na,nb->ab", left, right, preferred_element_type=jnp.float32)


def product_nt(left, right):
    return jnp.einsum("na,ba->nb", left, right, preferred_element_type=jnp.float32)


def column_sum(values):
    return jnp.sum(values.astype(jnp.float32), axis=0)


def placed_rows(term, before, after):
    widths = [(0, 0)] * term.ndim
    widths[1] = (before, after)
    return jnp.pad(term, widths)


def windows(kv_local):
    behind_win = kv_local
    ahead_win = kv_local
    for hop_level in range(HOPS):
        behind_win = jnp.concatenate(
            [passed_along(behind_win, "ctx", 2**hop_level), behind_win], axis=1
        )
        ahead_win = jnp.concatenate(
            [ahead_win, passed_along(ahead_win, "ctx", -(2**hop_level))], axis=1
        )
    return jnp.concatenate([behind_win, ahead_win[:, kv_local.shape[1] :]], axis=1)


def returns(grad_window, block_len):
    shard_span = 2**HOPS
    back_part = grad_window[:, : shard_span * block_len]
    fore_part = jnp.concatenate(
        [jnp.zeros_like(grad_window[:, :block_len]), grad_window[:, shard_span * block_len :]],
        axis=1,
    )
    for hop_level in reversed(range(HOPS)):
        piece_rows = 2**hop_level * block_len
        back_part = back_part[:, piece_rows:] + passed_along(
            for_sending(back_part[:, :piece_rows]), "ctx", -(2**hop_level)
        )
        fore_part = fore_part[:, :piece_rows] + passed_along(
            for_sending(fore_part[:, piece_rows:]), "ctx", 2**hop_level
        )
    return back_part + fore_part


def pair_views(query_seq, window_seq, pair_index):
    att_width = query_seq.shape[1]
    pair_width = 2 * HEAD_DIM
    start_col = pair_index * pair_width
    query_pair = query_seq[:, start_col : start_col + pair_width].reshape(-1, 2, HEAD_DIM)
    key_pair = window_seq[:, start_col : start_col + pair_width].reshape(-1, 2, HEAD_DIM)
    value_pair = window_seq[:, att_width + start_col : att_width + start_col + pair_width].reshape(
        -1, 2, HEAD_DIM
    )
    return (query_pair, key_pair, value_pair)


def pair_scores(query_pair, key_pair, same_doc):
    raw_scores = jnp.einsum(
        "qhd,khd->hqk", query_pair, key_pair, preferred_element_type=jnp.float32
    ) * HEAD_DIM ** (-0.5)
    return jnp.where(same_doc[None], raw_scores, -1000000000.0)


def attend_forward(inputs):
    query_seq, window_seq, query_seg, key_seg = inputs
    same_doc = query_seg[:, None] == key_seg[None, :]
    outputs = []
    log_sums = []
    for pair_index in range(query_seq.shape[1] // (2 * HEAD_DIM)):
        query_pair, key_pair, value_pair = pair_views(query_seq, window_seq, pair_index)
        scores = pair_scores(query_pair, key_pair, same_doc)
        row_max = jnp.max(scores, axis=-1, keepdims=True)
        exponent = jnp.exp(scores - row_max)
        row_sum = jnp.sum(exponent, axis=-1, keepdims=True)
        weights = (exponent / row_sum).astype(jnp.bfloat16)
        head_out = jnp.einsum(
            "hqk,khd->qhd", weights, value_pair, preferred_element_type=jnp.float32
        )
        outputs.append(head_out.reshape(head_out.shape[0], -1))
        log_sums.append(row_max + jnp.log(row_sum))
    return (jnp.concatenate(outputs, axis=1), jnp.concatenate(log_sums, axis=0))


def attend_backward(inputs):
    query_seq, window_seq, query_seg, key_seg, grad_seq, log_sums = inputs
    same_doc = query_seg[:, None] == key_seg[None, :]
    score_scale = HEAD_DIM ** (-0.5)
    pair_width = 2 * HEAD_DIM
    query_grads = []
    key_grads = []
    value_grads = []
    for pair_index in range(query_seq.shape[1] // pair_width):
        query_pair, key_pair, value_pair = pair_views(query_seq, window_seq, pair_index)
        scores = pair_scores(query_pair, key_pair, same_doc)
        probs = jnp.exp(scores - log_sums[2 * pair_index : 2 * pair_index + 2])
        weights = probs.astype(jnp.bfloat16)
        start_col = pair_index * pair_width
        grad_pair = grad_seq[:, start_col : start_col + pair_width].reshape(-1, 2, HEAD_DIM)
        grad_probs = jnp.einsum(
            "qhd,khd->hqk", grad_pair, value_pair, preferred_element_type=jnp.float32
        )
        inner_sum = jnp.sum(grad_probs * probs, axis=-1, keepdims=True)
        grad_scores = (probs * (grad_probs - inner_sum)).astype(jnp.bfloat16)
        grad_query = (
            jnp.einsum("hqk,khd->qhd", grad_scores, key_pair, preferred_element_type=jnp.float32)
            * score_scale
        )
        grad_key = (
            jnp.einsum("hqk,qhd->khd", grad_scores, query_pair, preferred_element_type=jnp.float32)
            * score_scale
        )
        grad_value = jnp.einsum(
            "hqk,qhd->khd", weights, grad_pair, preferred_element_type=jnp.float32
        )
        query_grads.append(grad_query.reshape(grad_query.shape[0], -1))
        key_grads.append(grad_key.reshape(grad_key.shape[0], -1))
        value_grads.append(grad_value.reshape(grad_value.shape[0], -1))
    return (jnp.concatenate(query_grads, axis=1), jnp.concatenate(key_grads + value_grads, axis=1))


def on_device(
    hidden_in,
    segment_ids,
    out_grad,
    query_w,
    query_b,
    key_w,
    value_w,
    value_b,
    depth_kernel,
    point_w,
    point_b,
    kernel_w,
    kernel_b,
    conv_w,
    conv_b,
    output_w,
    output_b,
    norm1_gain,
    norm1_bias,
    inner_w,
    inner_b,
    outer_w,
    outer_b,
    norm2_gain,
    norm2_bias,
):
    gathered = (
        lax.all_gather(query_w, "wsh", axis=0, tiled=True),
        lax.all_gather(query_b, "wsh", axis=0, tiled=True),
        lax.all_gather(key_w, "wsh", axis=0, tiled=True),
        lax.all_gather(value_w, "wsh", axis=0, tiled=True),
        lax.all_gather(value_b, "wsh", axis=0, tiled=True),
        lax.all_gather(depth_kernel, "wsh", axis=1, tiled=True),
        lax.all_gather(point_w, "wsh", axis=0, tiled=True),
        lax.all_gather(point_b, "wsh", axis=0, tiled=True),
        lax.all_gather(kernel_w, "wsh", axis=0, tiled=True),
        lax.all_gather(kernel_b, "wsh", axis=0, tiled=True),
        lax.all_gather(conv_w, "wsh", axis=0, tiled=True),
        lax.all_gather(conv_b, "wsh", axis=0, tiled=True),
        lax.all_gather(output_w, "wsh", axis=0, tiled=True),
        lax.all_gather(output_b, "wsh", axis=0, tiled=True),
        lax.all_gather(norm1_gain, "wsh", axis=0, tiled=True),
        lax.all_gather(norm1_bias, "wsh", axis=0, tiled=True),
        lax.all_gather(inner_w, "wsh", axis=1, tiled=True),
        lax.all_gather(inner_b, "wsh", axis=0, tiled=True),
        lax.all_gather(outer_w, "wsh", axis=1, tiled=True),
        lax.all_gather(outer_b, "wsh", axis=0, tiled=True),
        lax.all_gather(norm2_gain, "wsh", axis=0, tiled=True),
        lax.all_gather(norm2_bias, "wsh", axis=0, tiled=True),
    )
    (
        query_mat,
        query_vec,
        key_mat,
        value_mat,
        value_vec,
        depth_taps,
        point_mat,
        point_vec,
        kernel_mat,
        kernel_vec,
        conv_mat,
        conv_vec,
        output_mat,
        output_vec,
        gain_one,
        shift_one,
        inner_mat,
        inner_vec,
        outer_mat,
        outer_vec,
        gain_two,
        shift_two,
    ) = gathered
    micro_count, seq_local, block_len, model_width = hidden_in.shape
    seq_count = micro_count * seq_local
    row_count = seq_count * block_len
    att_width = query_mat.shape[1]
    half_taps = KERNEL // 2
    shard_span = 2**HOPS
    flat_rows = hidden_in.reshape(row_count, model_width)
    position = lax.axis_index("ctx")
    seg_rows = segment_ids.reshape(seq_count, segment_ids.shape[2])
    pad_rows = (shard_span - 1) * block_len
    seg_pad = jnp.pad(seg_rows, ((0, 0), (pad_rows, pad_rows)), constant_values=-1)
    own_seg = lax.dynamic_slice_in_dim(seg_pad, position * block_len + pad_rows, block_len, 1)
    key_seg = lax.dynamic_slice_in_dim(
        seg_pad, position * block_len, (2 * shard_span - 1) * block_len, 1
    )
    rim_seg = lax.dynamic_slice_in_dim(
        seg_pad, position * block_len + pad_rows - half_taps, block_len + 2 * half_taps, 1
    )
    tap_mask = jnp.stack(
        [rim_seg[:, offset : offset + block_len] == own_seg for offset in range(KERNEL)], axis=2
    ).astype(jnp.float32)
    rimmed = with_halo(
        hidden_in.reshape(seq_count, block_len, model_width), (("ctx", 1),), half_taps
    )
    queries = (product(flat_rows, query_mat) + query_vec).astype(jnp.bfloat16)
    kv_local = (
        jnp.concatenate(
            [product(flat_rows, key_mat), product(flat_rows, value_mat) + value_vec], axis=1
        )
        .astype(jnp.bfloat16)
        .reshape(seq_count, block_len, 2 * att_width)
    )
    window = windows(kv_local)
    depth_sum = sum(
        (
            depth_taps[offset].astype(jnp.float32)
            * rimmed[:, offset : offset + block_len]
            * tap_mask[:, :, offset : offset + 1]
            for offset in range(KERNEL)
        )
    )
    depth_low = depth_sum.astype(jnp.bfloat16).reshape(row_count, model_width)
    span_keys = product(depth_low, point_mat) + point_vec
    mixed_low = (span_keys * queries).astype(jnp.bfloat16)
    logits = (product(mixed_low, kernel_mat) + kernel_vec).reshape(
        seq_count, block_len, HEADS, KERNEL
    )
    kernels, kern_pull = jax.vjp(kernel_softmax, logits)
    conv_ext = (product(rimmed.reshape(-1, model_width), conv_mat) + conv_vec).reshape(
        seq_count, block_len + 2 * half_taps, HEADS, HEAD_DIM
    )
    convolved = sum(
        (
            (kernels[..., offset] * tap_mask[:, :, offset : offset + 1])[..., None]
            * conv_ext[:, offset : offset + block_len]
            for offset in range(KERNEL)
        )
    )
    query_blocks = queries.reshape(seq_count, block_len, att_width)
    attended, log_sums = lax.map(attend_forward, (query_blocks, window, own_seg, key_seg))
    joined = jnp.concatenate(
        [attended.reshape(row_count, att_width), convolved.reshape(row_count, att_width)], axis=1
    ).astype(jnp.bfloat16)
    branch = product(joined, output_mat) + output_vec
    normed, norm1_pull = jax.vjp(
        layer_norm, branch + flat_rows, gain_one.astype(jnp.float32), shift_one.astype(jnp.float32)
    )
    normed_low = normed.astype(jnp.bfloat16).reshape(row_count, GROUPS, -1)
    inner_pre = jnp.einsum(
        "ngd,gdf->ngf", normed_low, inner_mat, preferred_element_type=jnp.float32
    ) + inner_vec.reshape(GROUPS, -1)
    active, gelu_pull = jax.vjp(gelu_exact, inner_pre)
    active_low = active.astype(jnp.bfloat16)
    outer_out = (
        jnp.einsum("ngf,gfd->ngd", active_low, outer_mat, preferred_element_type=jnp.float32)
        + outer_vec.reshape(GROUPS, -1)
    ).reshape(row_count, model_width)
    final_out, norm2_pull = jax.vjp(
        layer_norm, outer_out + normed, gain_two.astype(jnp.float32), shift_two.astype(jnp.float32)
    )
    output = final_out.astype(jnp.bfloat16).reshape(hidden_in.shape)
    grad_sum2, grad_gain2, grad_shift2 = norm2_pull(
        out_grad.reshape(row_count, model_width).astype(jnp.float32)
    )
    grad_outer = grad_sum2.astype(jnp.bfloat16).reshape(row_count, GROUPS, -1)
    grad_outer_w = jnp.einsum(
        "ngf,ngd->gfd", active_low, grad_outer, preferred_element_type=jnp.float32
    )
    grad_outer_b = column_sum(grad_outer).reshape(-1)
    (grad_inner,) = gelu_pull(
        jnp.einsum("ngd,gfd->ngf", grad_outer, outer_mat, preferred_element_type=jnp.float32)
    )
    grad_inner = grad_inner.astype(jnp.bfloat16)
    grad_inner_w = jnp.einsum(
        "ngd,ngf->gdf", normed_low, grad_inner, preferred_element_type=jnp.float32
    )
    grad_inner_b = column_sum(grad_inner).reshape(-1)
    grad_normed = grad_sum2 + jnp.einsum(
        "ngf,gdf->ngd", grad_inner, inner_mat, preferred_element_type=jnp.float32
    ).reshape(row_count, model_width)
    grad_sum1, grad_gain1, grad_shift1 = norm1_pull(grad_normed)
    grad_branch = grad_sum1.astype(jnp.bfloat16)
    grad_output_w = product_tn(joined, grad_branch)
    grad_output_b = column_sum(grad_branch)
    grad_joined = product_nt(grad_branch, output_mat).astype(jnp.bfloat16)
    grad_attended = grad_joined[:, :att_width].reshape(seq_count, block_len, att_width)
    grad_conv = (
        grad_joined[:, att_width:]
        .astype(jnp.float32)
        .reshape(seq_count, block_len, HEADS, HEAD_DIM)
    )
    grad_kern_list = []
    ext_terms = []
    for offset in range(KERNEL):
        tap_weight = tap_mask[:, :, offset : offset + 1]
        grad_kern_list.append(
            jnp.sum(grad_conv * conv_ext[:, offset : offset + block_len], axis=-1) * tap_weight
        )
        ext_terms.append(
            placed_rows(
                (kernels[..., offset] * tap_weight)[..., None] * grad_conv,
                offset,
                2 * half_taps - offset,
            )
        )
    grad_ext = sum(ext_terms)
    (grad_logits,) = kern_pull(jnp.stack(grad_kern_list, axis=-1))
    grad_logits = grad_logits.reshape(row_count, HEADS * KERNEL).astype(jnp.bfloat16)
    grad_kernel_w = product_tn(mixed_low, grad_logits)
    grad_kernel_b = column_sum(grad_logits)
    grad_mixed = product_nt(grad_logits, kernel_mat)
    grad_spans = (grad_mixed * queries).astype(jnp.bfloat16)
    grad_query_conv = grad_mixed * span_keys
    grad_point_w = product_tn(depth_low, grad_spans)
    grad_point_b = column_sum(grad_spans)
    grad_depth = product_nt(grad_spans, point_mat).reshape(seq_count, block_len, model_width)
    grad_taps = []
    rim_terms = []
    for offset in range(KERNEL):
        masked_grad = grad_depth * tap_mask[:, :, offset : offset + 1]
        grad_taps.append(jnp.sum(masked_grad * rimmed[:, offset : offset + block_len], axis=(0, 1)))
        rim_terms.append(
            placed_rows(
                masked_grad * depth_taps[offset].astype(jnp.float32), offset, 2 * half_taps - offset
            )
        )
    grad_rim = sum(rim_terms)
    grad_depth_taps = jnp.stack(grad_taps, axis=0)
    rim_parts = jnp.concatenate([grad_ext.reshape(seq_count, -1, att_width), grad_rim], axis=2)
    edges = jnp.concatenate(
        [rim_parts[:, :half_taps], rim_parts[:, block_len + half_taps :]], axis=1
    )
    arrived = with_halo(edges.astype(jnp.bfloat16), (("ctx", 1),), half_taps).astype(edges.dtype)
    own_parts = (
        rim_parts[:, half_taps : half_taps + block_len]
        + placed_rows(arrived[:, :half_taps], 0, block_len - half_taps)
        + placed_rows(arrived[:, 3 * half_taps :], block_len - half_taps, 0)
    )
    grad_conv_vals = own_parts[..., :att_width].reshape(row_count, att_width).astype(jnp.bfloat16)
    grad_conv_w = product_tn(flat_rows, grad_conv_vals)
    grad_conv_b = column_sum(grad_conv_vals)
    grad_query_att, grad_window = lax.map(
        attend_backward, (query_blocks, window, own_seg, key_seg, grad_attended, log_sums)
    )
    grad_kv = returns(grad_window, block_len).reshape(row_count, 2 * att_width)
    grad_keys = grad_kv[:, :att_width].astype(jnp.bfloat16)
    grad_values = grad_kv[:, att_width:].astype(jnp.bfloat16)
    grad_queries = (grad_query_att.reshape(row_count, att_width) + grad_query_conv).astype(
        jnp.bfloat16
    )
    grad_query_w = product_tn(flat_rows, grad_queries)
    grad_query_b = column_sum(grad_queries)
    grad_key_w = product_tn(flat_rows, grad_keys)
    grad_value_w = product_tn(flat_rows, grad_values)
    grad_value_b = column_sum(grad_values)
    grad_input = (
        grad_sum1
        + product_nt(grad_queries, query_mat)
        + product_nt(grad_keys, key_mat)
        + product_nt(grad_values, value_mat)
        + product_nt(grad_conv_vals, conv_mat)
        + own_parts[..., att_width:].reshape(row_count, model_width)
    ).reshape(hidden_in.shape)
    summed = lax.psum(
        (
            grad_query_w,
            grad_query_b,
            grad_key_w,
            grad_value_w,
            grad_value_b,
            grad_depth_taps,
            grad_point_w,
            grad_point_b,
            grad_kernel_w,
            grad_kernel_b,
            grad_conv_w,
            grad_conv_b,
            grad_output_w,
            grad_output_b,
            grad_gain1,
            grad_shift1,
            grad_inner_w,
            grad_inner_b,
            grad_outer_w,
            grad_outer_b,
            grad_gain2,
            grad_shift2,
        ),
        "ctx",
    )
    shares = (
        lax.psum_scatter(
            summed[0].astype(jnp.bfloat16), "wsh", scatter_dimension=0, tiled=True
        ).astype(jnp.float32),
        lax.psum_scatter(
            summed[1].astype(jnp.bfloat16), "wsh", scatter_dimension=0, tiled=True
        ).astype(jnp.float32),
        lax.psum_scatter(
            summed[2].astype(jnp.bfloat16), "wsh", scatter_dimension=0, tiled=True
        ).astype(jnp.float32),
        lax.psum_scatter(
            summed[3].astype(jnp.bfloat16), "wsh", scatter_dimension=0, tiled=True
        ).astype(jnp.float32),
        lax.psum_scatter(
            summed[4].astype(jnp.bfloat16), "wsh", scatter_dimension=0, tiled=True
        ).astype(jnp.float32),
        lax.psum_scatter(
            summed[5].astype(jnp.bfloat16), "wsh", scatter_dimension=1, tiled=True
        ).astype(jnp.float32),
        lax.psum_scatter(
            summed[6].astype(jnp.bfloat16), "wsh", scatter_dimension=0, tiled=True
        ).astype(jnp.float32),
        lax.psum_scatter(
            summed[7].astype(jnp.bfloat16), "wsh", scatter_dimension=0, tiled=True
        ).astype(jnp.float32),
        lax.psum_scatter(
            summed[8].astype(jnp.bfloat16), "wsh", scatter_dimension=0, tiled=True
        ).astype(jnp.float32),
        lax.psum_scatter(
            summed[9].astype(jnp.bfloat16), "wsh", scatter_dimension=0, tiled=True
        ).astype(jnp.float32),
        lax.psum_scatter(
            summed[10].astype(jnp.bfloat16), "wsh", scatter_dimension=0, tiled=True
        ).astype(jnp.float32),
        lax.psum_scatter(
            summed[11].astype(jnp.bfloat16), "wsh", scatter_dimension=0, tiled=True
        ).astype(jnp.float32),
        lax.psum_scatter(
            summed[12].astype(jnp.bfloat16), "wsh", scatter_dimension=0, tiled=True
        ).astype(jnp.float32),
        lax.psum_scatter(
            summed[13].astype(jnp.bfloat16), "wsh", scatter_dimension=0, tiled=True
        ).astype(jnp.float32),
        lax.psum_scatter(
            summed[14].astype(jnp.bfloat16), "wsh", scatter_dimension=0, tiled=True
        ).astype(jnp.float32),
        lax.psum_scatter(
            summed[15].astype(jnp.bfloat16), "wsh", scatter_dimension=0, tiled=True
        ).astype(jnp.float32),
        lax.psum_scatter(
            summed[16].astype(jnp.bfloat16), "wsh", scatter_dimension=1, tiled=True
        ).astype(jnp.float32),
        lax.psum_scatter(
            summed[17].astype(jnp.bfloat16), "wsh", scatter_dimension=0, tiled=True
        ).astype(jnp.float32),
        lax.psum_scatter(
            summed[18].astype(jnp.bfloat16), "wsh", scatter_dimension=1, tiled=True
        ).astype(jnp.float32),
        lax.psum_scatter(
            summed[19].astype(jnp.bfloat16), "wsh", scatter_dimension=0, tiled=True
        ).astype(jnp.float32),
        lax.psum_scatter(
            summed[20].astype(jnp.bfloat16), "wsh", scatter_dimension=0, tiled=True
        ).astype(jnp.float32),
        lax.psum_scatter(
            summed[21].astype(jnp.bfloat16), "wsh", scatter_dimension=0, tiled=True
        ).astype(jnp.float32),
    )
    return (output, grad_input) + tuple(shares)


def solution(mesh):
    in_specs = (
        P(None, "wsh", "ctx", None),
        P(None, "wsh", None),
        P(None, "wsh", "ctx", None),
        P("wsh", None),
        P("wsh"),
        P("wsh", None),
        P("wsh", None),
        P("wsh"),
        P(None, "wsh"),
        P("wsh", None),
        P("wsh"),
        P("wsh", None),
        P("wsh"),
        P("wsh", None),
        P("wsh"),
        P("wsh", None),
        P("wsh"),
        P("wsh"),
        P("wsh"),
        P(None, "wsh", None),
        P("wsh"),
        P(None, "wsh", None),
        P("wsh"),
        P("wsh"),
        P("wsh"),
    )
    out_specs = (
        P(None, "wsh", "ctx", None),
        P(None, "wsh", "ctx", None),
        P("wsh", None),
        P("wsh"),
        P("wsh", None),
        P("wsh", None),
        P("wsh"),
        P(None, "wsh"),
        P("wsh", None),
        P("wsh"),
        P("wsh", None),
        P("wsh"),
        P("wsh", None),
        P("wsh"),
        P("wsh", None),
        P("wsh"),
        P("wsh"),
        P("wsh"),
        P(None, "wsh", None),
        P("wsh"),
        P(None, "wsh", None),
        P("wsh"),
        P("wsh"),
        P("wsh"),
    )
    return jax.shard_map(
        on_device, mesh=mesh, in_specs=in_specs, out_specs=out_specs, check_vma=False
    )
```

profile of v0, /device:TPU:0, one launch (start us, length us, event | category | flops | bytes accessed | tf_op | source)
XLA Modules:
  0.0 1679.0 jit_solution(18255233960099745150)
XLA Ops:
  15.6 6.4 all-reduce.41
  23.2 16.4 all_gather.67
  41.0 7.8 all_gather.66
  116.0 8.3 all_gather.69
  135.3 8.3 all_gather.72
  143.6 7.7 all_gather.76
  156.4 6.7 collective-permute-start.1
  163.3 8.7 fusion.58
  187.2 13.4 add_convert_fusion.3
  202.7 87.0 %collective-permute-done.1 = bf16[2,1024,768]{1,2,0:T(8,128)(2,1)} collective-permute-done((bf16[2,1024,768]{1,2,0:T(8,128)(2,1)}, bf16[2,1024,768]{1,2,0:T(8,128)(2,1)}, u32[]{:S(2)}, u32[]{:S(2)}) %collective-permute-start.1) | collective-permute-done | bytes 3145760 | tf_op jit(solution)/shard_map/ppermute | solution.py:16
  301.4 138.8 %while.26 = (s32[]{:T(128)}, bf16[2,512,384]{2,1,0:T(8,128)(2,1)S(1)}, f32[2,6,512,1]{2,1,3,0:T(8,128)S(1)}, bf16[2,3584,768]{1,2,0:T(8,128)(2,1)}, s32[2,512]{1...) while((s32[]{:T(128)}, bf16[2,512,384]{2,1,0:T(8,128)(2,1)S(1)}, ...), condition=%wide.region_7.8_spmd.clone, body=%wide.region_0.7_spmd.sunk.clone | while | flops 2953710592 | bytes 239775984 | solution.py:317
  307.4 7.3 fusion.347
  314.7 6.9 fusion.348
  321.6 17.8 %fusion.349 = (f32[2,512]{1,0:T(2,128)S(1)}, f32[2,512]{1,0:T(2,128)S(1)}, f32[2,512]{1,0:T(2,128)S(1)}, f32[2,512,3584]{2,1,0:T(8,128)}) fusion(f32[2,512,3584]{2,1,0:T(8,128)} %get-tuple-element.660, f32[2,512]{1,0:T(2,128)S(1)} %get-tuple-element.661, pred[512,3584]{1,0:T(8,128)(4,1)S(1)} %broadcast_compare_fusion.6, ...), kind=kOutput, calls=%fused_computation.12.clone.1.clone | convolution fusion | flops 506459136 | bytes 46940160 | tf_op jit(solution)/shard_map/while/body/eval_jaxpr/qhd,khd->hqk/dot_general | solution.py:120
  339.4 7.6 fusion.353
  349.1 9.8 fusion.350
  359.0 7.2 fusion.352
  376.5 7.3 fusion.347
  383.8 6.9 fusion.348
  390.7 17.8 %fusion.349 = (f32[2,512]{1,0:T(2,128)S(1)}, f32[2,512]{1,0:T(2,128)S(1)}, f32[2,512]{1,0:T(2,128)S(1)}, f32[2,512,3584]{2,1,0:T(8,128)}) fusion(f32[2,512,3584]{2,1,0:T(8,128)} %get-tuple-element.660, f32[2,512]{1,0:T(2,128)S(1)} %get-tuple-element.661, pred[512,3584]{1,0:T(8,128)(4,1)S(1)} %broadcast_compare_fusion.6, ...), kind=kOutput, calls=%fused_computation.12.clone.1.clone | convolution fusion | flops 506459136 | bytes 46940160 | tf_op jit(solution)/shard_map/while/body/eval_jaxpr/qhd,khd->hqk/dot_general | solution.py:120
  408.6 7.6 fusion.353
  418.2 9.8 fusion.350
  428.1 7.2 fusion.352
  448.0 33.6 %fusion.31 = (bf16[1024,2,1536]{2,0,1:T(8,128)(2,1)}, f32[1024,2,1536]{2,0,1:T(8,128)}, f32[2,1024,1536]{2,1,0:T(8,128)}) fusion(f32[2,1536]{1,0:T(2,128)S(1)} %bitcast.802, bf16[1024,2,384]{0,2,1:T(8,128)(2,1)} %bitcast.783, bf16[2,384,1536]{2,1,0:T(8,128)(2,1)} %all-gather.14.cloned.1.call-done), kind=kOutput, calls=%fused_computation.92 | convolution fusion | flops 2623537152 | bytes 35401728 | tf_op jit(solution)/shard_map/ngd,gdf->ngf/dot_general | solution.py:326
  494.9 16.5 convert_reduce_fusion
  525.0 297.8 %while.27 = (s32[]{:T(128)}, f32[2,512,384]{2,1,0:T(8,128)}, f32[2,3584,768]{2,1,0:T(8,128)}, bf16[2,3584,768]{1,2,0:T(8,128)(2,1)}, s32[2,512]{1,0:T(2,128)S(1)...) while((s32[]{:T(128)}, f32[2,512,384]{2,1,0:T(8,128)}, ...), condition=%wide.region_22.23_spmd.clone, body=%wide.region_18.22_spmd.sunk.clone | while | flops 7149319168 | bytes 534229952 | solution.py:419
  561.7 7.3 multiply_reduce_fusion.25
  569.1 7.0 multiply_convert_fusion.11
  587.7 7.2 subtract_exponential_fusion.15
  594.9 7.9 fusion.388
  602.8 12.5 multiply_reduce_fusion.27
  615.3 10.5 multiply_convert_fusion.13
  631.8 7.3 multiply_reduce_fusion.26
  639.2 7.1 multiply_convert_fusion.12
  657.6 12.2 copy.275
  671.3 9.5 constant_dynamic-update-slice_fusion.58
  696.4 7.3 multiply_reduce_fusion.25
  703.7 7.0 multiply_convert_fusion.11
  722.3 7.2 subtract_exponential_fusion.15
  729.5 7.9 fusion.388
  737.4 12.5 multiply_reduce_fusion.27
  749.9 10.5 multiply_convert_fusion.13
  766.5 7.3 multiply_reduce_fusion.26
  773.8 7.1 multiply_convert_fusion.12
  792.2 12.2 copy.275
  805.9 9.5 constant_dynamic-update-slice_fusion.58
  828.8 19.7 %multiply_reduce_fusion.9 = (f32[2,512,6]{1,0,2:T(2,128)S(1)}, f32[2,512,6]{1,0,2:T(2,128)S(1)}, f32[2,512,6]{1,0,2:T(2,128)S(1)}, f32[2,512,6]{1,0,2:T(2,128)S(...) fusion(f32[2,512,6,64]{1,0,3,2:T(2,128)S(1)} %reshape.639, ...), kind=kLoop, calls=%fused_computation.229 | loop fusion | flops 10561536 | bytes 30326784 | tf_op jit(solution)/shard_map/reduce_sum | solution.py:374
  849.3 17.3 %pad_add_fusion.1 = f32[2,520,6,64]{1,0,3,2:T(2,128)} fusion(f32[2,512,6,64]{1,0,3,2:T(2,128)S(1)} %get-tuple-element.425, f32[2,512,6,64]{1,0,3,2:T(2,128)S(1)} %get-tuple-element.424, f32[2,512,6,64]{1,0,3,2:T(2,128)S(1)} %get-tuple-element.423, f32[2,512,6,64]{1,0,3,2:T(2,128)S(1)} %get-tuple-element.422, f32[2,512,6,64]{1,0,3,2:T(2,128)S(1)} %get-tuple-element.421, ...), kind=kLoop, calls=%fused_computation.204 | loop fusion | flops 3194880 | bytes 15753216 | tf_op jit(solution)/shard_map/add | solution.py:383
  870.3 8.0 convert.52
  883.4 6.7 collective-permute-start.8
  906.4 5.9 pad_add_fusion
  914.0 7.9 slice.447
  936.9 7.0 fusion.145
  943.9 7.2 fusion.144
  958.3 57.8 %collective-permute-done.8 = bf16[2,1024,768]{2,1,0:T(8,128)(2,1)} collective-permute-done((bf16[2,1024,768]{2,1,0:T(8,128)(2,1)}, bf16[2,1024,768]{2,1,0:T(8,128)(2,1)}, u32[]{:S(2)}, u32[]{:S(2)}) %collective-permute-start.8) | collective-permute-done | bytes 3145760 | tf_op jit(solution)/shard_map/ppermute | solution.py:16
  1040.9 403.7 %all-reduce.43 = (bf16[768,384]{0,1:T(8,128)(2,1)}, bf16[768,384]{0,1:T(8,128)(2,1)S(1)}, bf16[768,384]{0,1:T(8,128)(2,1)S(1)}, bf16[768,384]{0,1:T(8,128)(2,1)S...) all-reduce(f32[768,384]{0,1:T(8,128)S(1)} %copy-done.62, ...), channel_id=1, replica_groups=mesh['ctx'=16,'wsh'=2] {'ctx'}, use_global_device_ids=true, to_apply=%region_33.34 | all-reduce | flops 4460598 | bytes 26763588 | tf_op jit(solution)/shard_map/psum | solution.py:441
  1479.8 8.4 all-reduce.40
  1500.6 16.4 reduce-scatter.33.cloned.1.call-done
  1519.1 15.9 reduce-scatter.35.cloned.1.call-done
  1537.2 15.5 reduce-scatter.41.cloned.1.call-done
  1554.9 15.2 reduce-scatter.23.cloned.1.call-done
  1571.9 22.9 %reduce-scatter.25.cloned.1.call-done = bf16[384,768]{1,0:T(8,128)(2,1)} async-done(((bf16[768,768]{1,0:T(8,128)(2,1)}), bf16[384,768]{1,0:T(8,128)(2,1)}) %reduce-scatter.25.cloned.1.call-update) | async-done | bytes 589840 | tf_op jit(solution)/shard_map/reduce_scatter | solution.py:505
  1596.9 34.7 %reduce-scatter.29.cloned.1.call-done = bf16[2,768,384]{2,1,0:T(8,128)(2,1)} async-done(((bf16[2,1536,384]{2,1,0:T(8,128)(2,1)}), bf16[2,768,384]{2,1,0:T(8,128)(2,1)}) %reduce-scatter.29.cloned.1.call-update) | async-done | bytes 1179664 | tf_op jit(solution)/shard_map/reduce_scatter | solution.py:523
  1634.5 34.8 %reduce-scatter.27.cloned.1.call-done = bf16[2,192,1536]{2,1,0:T(8,128)(2,1)} async-done(((bf16[2,384,1536]{2,1,0:T(8,128)(2,1)}), bf16[2,192,1536]{2,1,0:T(8,128)(2,1)}) %reduce-scatter.27.cloned.1.call-update) | async-done | bytes 1179664 | tf_op jit(solution)/shard_map/reduce_scatter | solution.py:517
  (831 shorter events, 411.5 us)
Async XLA Ops:
  7.2 32.5 %copy-start.5 = (bf16[2,1,512,768]{3,2,1,0:T(8,128)(2,1)S(1)}, bf16[2,1,512,768]{3,2,1,0:T(8,128)(2,1)}, u32[]{:S(2)}) copy-start(bf16[2,1,512,768]{3,2,1,0:T(8,128)(2,1)} %param.29) | copy-start | bytes 4718596
  7.2 433.1 %all-gather.12.cloned.1.call-start = ((), (), s32[]{:S(2)}) async-start(), calls=%async_computation.10 | async-start | bytes 1769472 | tf_op jit(solution)/shard_map/all_gather | solution.py:223
  7.9 440.1 %all-gather.14.cloned.1.call-start = ((), (), s32[]{:S(2)}) async-start(), calls=%async_computation.11 | async-start | bytes 3538944 | tf_op jit(solution)/shard_map/all_gather | solution.py:227
  8.7 473.0 %all-gather.16.cloned.1.call-start = ((), (), s32[]{:S(2)}) async-start(), calls=%async_computation.12 | async-start | bytes 3538944 | tf_op jit(solution)/shard_map/all_gather | solution.py:229
  51.8 100.2 %collective-permute-start.2 = (bf16[2,512,768]{1,2,0:T(8,128)(2,1)}, bf16[2,512,768]{1,2,0:T(8,128)(2,1)}, u32[]{:S(2)}, u32[]{:S(2)}) collective-permute-start(bf16[2,512,768]{1,2,0:T(8,128)(2,1)} %pad_maximum_fusion.5), channel_id=1, source_target_pairs={{2,0},{4,2},{6,4},{8,6},{10,8},{12,10},{14,12},{16,14},{18,16},{20... | collective-permute-start | bytes 4718600 | tf_op jit(solution)/shard_map/ppermute | solution.py:16
  53.1 98.9 %collective-permute-start = (bf16[2,512,768]{1,2,0:T(8,128)(2,1)}, bf16[2,512,768]{1,2,0:T(8,128)(2,1)}, u32[]{:S(2)}, u32[]{:S(2)}) collective-permute-start(bf16[2,512,768]{1,2,0:T(8,128)(2,1)} %pad_maximum_fusion.5), channel_id=1, source_target_pairs={{0,2},{2,4},{4,6},{6,8},{8,10},{10,12},{12,14},{14,16},{16,18},{18... | collective-permute-start | bytes 4718600 | tf_op jit(solution)/shard_map/ppermute | solution.py:16
  57.9 105.2 %collective-permute-start.4 = (bf16[2,4,768]{2,1,0:T(4,128)(2,1)}, bf16[2,4,768]{2,1,0:T(4,128)(2,1)}, u32[]{:S(2)}, u32[]{:S(2)}) collective-permute-start(bf16[2,4,768]{2,1,0:T(4,128)(2,1)} %get-tuple-element.428), channel_id=1, source_target_pairs={{0,2},{2,4},{4,6},{6,8},{8,10},{10,12},{12,14},{14,16},{16,18},{18... | collective-permute-start | bytes 36872 | tf_op jit(solution)/shard_map/ppermute | solution.py:32
  60.4 41.5 %copy-start.59 = (bf16[2,1,512,768]{3,2,1,0:T(8,128)(2,1)S(1)}, bf16[2,1,512,768]{3,2,1,0:T(8,128)(2,1)}, u32[]{:S(2)}) copy-start(bf16[2,1,512,768]{3,2,1,0:T(8,128)(2,1)} %param.31) | copy-start | bytes 4718596
  60.4 102.7 %collective-permute-start.5 = (bf16[2,4,768]{2,1,0:T(4,128)(2,1)}, bf16[2,4,768]{2,1,0:T(4,128)(2,1)}, u32[]{:S(2)}, u32[]{:S(2)}) collective-permute-start(bf16[2,4,768]{2,1,0:T(4,128)(2,1)} %get-tuple-element.429), channel_id=1, source_target_pairs={{2,0},{4,2},{6,4},{8,6},{10,8},{12,10},{14,12},{16,14},{18,16},{20... | collective-permute-start | bytes 36872 | tf_op jit(solution)/shard_map/ppermute | solution.py:35
  64.2 38.6 %copy-start.180 = (bf16[1536]{0:T(1024)(128)(2,1)S(1)}, bf16[1536]{0:T(1024)(128)(2,1)}, u32[]{:S(2)}) copy-start(bf16[1536]{0:T(1024)(128)(2,1)} %param.49) | copy-start | bytes 9220
  64.2 43.7 %copy-start.166 = (bf16[192,54]{0,1:T(8,128)(2,1)S(1)}, bf16[192,54]{0,1:T(8,128)(2,1)}, u32[]{:S(2)}) copy-start(bf16[192,54]{0,1:T(8,128)(2,1)} %param.40) | copy-start | bytes 62212
  64.2 49.7 %copy-start.141 = (s32[2,1,8192]{2,1,0:T(1,128)S(1)}, s32[2,1,8192]{2,1,0:T(1,128)}, u32[]{:S(2)}) copy-start(s32[2,1,8192]{2,1,0:T(1,128)} %param.30) | copy-start | bytes 196612
  64.3 51.7 %copy-start.97 = (bf16[384,384]{1,0:T(8,128)(2,1)S(1)}, bf16[384,384]{1,0:T(8,128)(2,1)}, u32[]{:S(2)}) copy-start(bf16[384,384]{1,0:T(8,128)(2,1)} %param.32) | copy-start | bytes 884740
  64.3 1428.4 %reduce-scatter.37.cloned.1.call-start = ((), (), s32[]{:S(2)}) async-start(), calls=%async_computation.20 | async-start | bytes 294912
  115.4 71.5 %copy-start.108 = (f32[2,512]{1,0:T(2,128)}, f32[2,512]{1,0:T(2,128)S(1)}, u32[]{:S(2)}) copy-start(f32[2,512]{1,0:T(2,128)S(1)} %get-tuple-element.442) | copy-start | bytes 12292
  115.4 71.5 %copy-start.110 = (f32[2,512]{1,0:T(2,128)}, f32[2,512]{1,0:T(2,128)S(1)}, u32[]{:S(2)}) copy-start(f32[2,512]{1,0:T(2,128)S(1)} %get-tuple-element.443) | copy-start | bytes 12292
  115.4 71.5 %copy-start.112 = (f32[2,512]{1,0:T(2,128)}, f32[2,512]{1,0:T(2,128)S(1)}, u32[]{:S(2)}) copy-start(f32[2,512]{1,0:T(2,128)S(1)} %get-tuple-element.444) | copy-start | bytes 12292
  126.0 48.9 %copy-start.44 = (bf16[1024,384]{1,0:T(8,128)(2,1)}, bf16[1024,384]{1,0:T(8,128)(2,1)S(1)}, u32[]{:S(2)}) copy-start(bf16[1024,384]{1,0:T(8,128)(2,1)S(1)} %add_convert_fusion.4) | copy-start | bytes 2359300
  129.4 22.6 %copy-start.49 = (bf16[2,512,384]{1,2,0:T(8,128)(2,1)S(1)}, bf16[2,512,384]{1,2,0:T(8,128)(2,1)}, u32[]{:S(2)}) copy-start(bf16[2,512,384]{1,2,0:T(8,128)(2,1)} %copy-done.48) | copy-start | bytes 2359300
  129.4 22.6 %copy-start.56 = (bf16[2,512,384]{1,2,0:T(8,128)(2,1)S(1)}, bf16[2,512,384]{1,2,0:T(8,128)(2,1)}, u32[]{:S(2)}) copy-start(bf16[2,512,384]{1,2,0:T(8,128)(2,1)} %copy-done.55) | copy-start | bytes 2359300
  134.2 28.9 %copy-start.142 = (f32[768]{0:T(1024)}, f32[768]{0:T(1024)S(1)}, u32[]{:S(2)}) copy-start(f32[768]{0:T(1024)S(1)} %get-tuple-element.261) | copy-start | bytes 9220
  134.3 28.9 %copy-start.144 = (f32[768]{0:T(1024)}, f32[768]{0:T(1024)S(1)}, u32[]{:S(2)}) copy-start(f32[768]{0:T(1024)S(1)} %get-tuple-element.267) | copy-start | bytes 9220
  134.3 28.9 %copy-start.146 = (f32[768]{0:T(1024)}, f32[768]{0:T(1024)S(1)}, u32[]{:S(2)}) copy-start(f32[768]{0:T(1024)S(1)} %get-tuple-element.268) | copy-start | bytes 9220
  134.3 28.9 %copy-start.148 = (f32[768]{0:T(1024)}, f32[768]{0:T(1024)S(1)}, u32[]{:S(2)}) copy-start(f32[768]{0:T(1024)S(1)} %get-tuple-element.269) | copy-start | bytes 9220
  134.3 28.9 %copy-start.150 = (f32[768]{0:T(1024)}, f32[768]{0:T(1024)S(1)}, u32[]{:S(2)}) copy-start(f32[768]{0:T(1024)S(1)} %get-tuple-element.262) | copy-start | bytes 9220
  134.3 28.9 %copy-start.152 = (f32[768]{0:T(1024)}, f32[768]{0:T(1024)S(1)}, u32[]{:S(2)}) copy-start(f32[768]{0:T(1024)S(1)} %get-tuple-element.263) | copy-start | bytes 9220
  134.3 28.9 %copy-start.154 = (f32[768]{0:T(1024)}, f32[768]{0:T(1024)S(1)}, u32[]{:S(2)}) copy-start(f32[768]{0:T(1024)S(1)} %get-tuple-element.264) | copy-start | bytes 9220
  134.3 28.9 %copy-start.156 = (f32[768]{0:T(1024)}, f32[768]{0:T(1024)S(1)}, u32[]{:S(2)}) copy-start(f32[768]{0:T(1024)S(1)} %get-tuple-element.265) | copy-start | bytes 9220
  134.3 28.9 %copy-start.158 = (f32[768]{0:T(1024)}, f32[768]{0:T(1024)S(1)}, u32[]{:S(2)}) copy-start(f32[768]{0:T(1024)S(1)} %get-tuple-element.266) | copy-start | bytes 9220
  143.6 28.4 %copy-start.69 = (bf16[768,384]{1,0:T(8,128)(2,1)}, bf16[768,384]{1,0:T(8,128)(2,1)S(1)}, u32[]{:S(2)}) copy-start(bf16[768,384]{1,0:T(8,128)(2,1)S(1)} %all_gather.72) | copy-start | bytes 1769476
  156.4 133.2 %collective-permute-start.1 = (bf16[2,1024,768]{1,2,0:T(8,128)(2,1)}, bf16[2,1024,768]{1,2,0:T(8,128)(2,1)}, u32[]{:S(2)}, u32[]{:S(2)}) collective-permute-start(bf16[2,1024,768]{1,2,0:T(8,128)(2,1)} %get-tuple-element.427), channel_id=1, source_target_pairs={{0,4},{2,6},{4,8},{6,10},{8,12},{10,14},{12,16},{14,18},{16,20},{1... | collective-permute-start | bytes 9437192 | tf_op jit(solution)/shard_map/ppermute | solution.py:16
  173.2 121.9 %collective-permute-start.3 = (bf16[2,1024,768]{1,2,0:T(8,128)(2,1)}, bf16[2,1024,768]{1,2,0:T(8,128)(2,1)}, u32[]{:S(2)}, u32[]{:S(2)}) collective-permute-start(bf16[2,1024,768]{1,2,0:T(8,128)(2,1)} %get-tuple-element.426), channel_id=1, source_target_pairs={{4,0},{6,2},{8,4},{10,6},{12,8},{14,10},{16,12},{18,14},{20,16},{2... | collective-permute-start | bytes 9437192 | tf_op jit(solution)/shard_map/ppermute | solution.py:16
  202.7 90.7 %copy-start.50 = (bf16[2,512,384]{1,2,0:T(8,128)(2,1)S(1)}, bf16[2,512,384]{1,2,0:T(8,128)(2,1)}, u32[]{:S(2)}) copy-start(bf16[2,512,384]{1,2,0:T(8,128)(2,1)} %copy-done.48) | copy-start | bytes 2359300
  202.7 90.7 %copy-start.57 = (bf16[2,512,384]{1,2,0:T(8,128)(2,1)S(1)}, bf16[2,512,384]{1,2,0:T(8,128)(2,1)}, u32[]{:S(2)}) copy-start(bf16[2,512,384]{1,2,0:T(8,128)(2,1)} %copy-done.55) | copy-start | bytes 2359300
  301.4 140.0 %copy-start.179 = (f32[768]{0:T(1024)S(1)}, f32[768]{0:T(1024)}, u32[]{:S(2)}) copy-start(f32[768]{0:T(1024)} %reshape.672) | copy-start | bytes 9220
  448.0 33.6 %copy-start.181 = (f32[2,1,384]{2,0,1:T(2,128)S(1)}, f32[2,1,384]{2,0,1:T(2,128)}, u32[]{:S(2)}) copy-start(f32[2,1,384]{2,0,1:T(2,128)} %copy.263) | copy-start | bytes 9220
  828.7 20.0 %copy-start.138 = (f32[2,512]{1,0:T(2,128)S(1)}, f32[2,512]{1,0:T(2,128)}, u32[]{:S(2)}) copy-start(f32[2,512]{1,0:T(2,128)} %get-tuple-element.446) | copy-start | bytes 12292
  828.7 20.0 %copy-start.116 = (f32[2,512]{1,0:T(2,128)S(1)}, f32[2,512]{1,0:T(2,128)}, u32[]{:S(2)}) copy-start(f32[2,512]{1,0:T(2,128)} %get-tuple-element.445) | copy-start | bytes 12292
  828.7 20.0 %copy-start.113 = (f32[2,512]{1,0:T(2,128)S(1)}, f32[2,512]{1,0:T(2,128)}, u32[]{:S(2)}) copy-start(f32[2,512]{1,0:T(2,128)} %copy-done.112) | copy-start | bytes 12292
  828.7 20.0 %copy-start.111 = (f32[2,512]{1,0:T(2,128)S(1)}, f32[2,512]{1,0:T(2,128)}, u32[]{:S(2)}) copy-start(f32[2,512]{1,0:T(2,128)} %copy-done.110) | copy-start | bytes 12292
  828.7 20.0 %copy-start.109 = (f32[2,512]{1,0:T(2,128)S(1)}, f32[2,512]{1,0:T(2,128)}, u32[]{:S(2)}) copy-start(f32[2,512]{1,0:T(2,128)} %copy-done.108) | copy-start | bytes 12292
  828.7 20.1 %copy-start.61 = (f32[2,512,6,9]{1,0,3,2:T(2,128)S(1)}, f32[2,512,6,9]{1,0,3,2:T(2,128)}, u32[]{:S(2)}) copy-start(f32[2,512,6,9]{1,0,3,2:T(2,128)} %copy-done.60) | copy-start | bytes 663556
  828.8 20.1 %copy-start.92 = (f32[2,512,6]{1,0,2:T(2,128)S(1)}, f32[2,512,6]{1,0,2:T(2,128)}, u32[]{:S(2)}) copy-start(f32[2,512,6]{1,0,2:T(2,128)} %copy-done.91) | copy-start | bytes 73732
  828.8 20.1 %copy-start.140 = (f32[2,512,6]{1,0,2:T(2,128)S(1)}, f32[2,512,6]{1,0,2:T(2,128)}, u32[]{:S(2)}) copy-start(f32[2,512,6]{1,0,2:T(2,128)} %multiply_divide_fusion) | copy-start | bytes 73732
  828.8 20.3 %copy-start.94 = (f32[2,512,6]{1,0,2:T(2,128)S(1)}, f32[2,512,6]{1,0,2:T(2,128)}, u32[]{:S(2)}) copy-start(f32[2,512,6]{1,0,2:T(2,128)} %copy-done.93) | copy-start | bytes 73732
  882.0 69.1 %collective-permute-start.6 = (bf16[2,1024,768]{2,1,0:T(8,128)(2,1)}, bf16[2,1024,768]{2,1,0:T(8,128)(2,1)}, u32[]{:S(2)}, u32[]{:S(2)}) collective-permute-start(bf16[2,1024,768]{2,1,0:T(8,128)(2,1)} %get-tuple-element.399), channel_id=1, source_target_pairs={{4,0},{6,2},{8,4},{10,6},{12,8},{14,10},{16,12},{18,14},{20,16},{2... | collective-permute-start | bytes 9437192 | tf_op jit(solution)/shard_map/ppermute | solution.py:16
  883.4 132.6 %collective-permute-start.8 = (bf16[2,1024,768]{2,1,0:T(8,128)(2,1)}, bf16[2,1024,768]{2,1,0:T(8,128)(2,1)}, u32[]{:S(2)}, u32[]{:S(2)}) collective-permute-start(bf16[2,1024,768]{2,1,0:T(8,128)(2,1)} %get-tuple-element.400), channel_id=1, source_target_pairs={{0,4},{2,6},{4,8},{6,10},{8,12},{10,14},{12,16},{14,18},{16,20},{1... | collective-permute-start | bytes 9437192 | tf_op jit(solution)/shard_map/ppermute | solution.py:16
  925.5 100.5 %collective-permute-start.10 = (bf16[2,4,1152]{2,1,0:T(4,128)(2,1)S(1)}, bf16[2,4,1152]{2,1,0:T(4,128)(2,1)S(1)}, u32[]{:S(2)}, u32[]{:S(2)}) collective-permute-start(bf16[2,4,1152]{2,1,0:T(4,128)(2,1)S(1)} %get-tuple-element.411), channel_id=1, source_target_pairs={{0,2},{2,4},{4,6},{6,8},{8,10},{10,12},{12,14},{14,16},{16,18},{18... | collective-permute-start | bytes 55304 | tf_op jit(solution)/shard_map/ppermute | solution.py:32
  926.9 99.1 %collective-permute-start.11 = (bf16[2,4,1152]{2,1,0:T(4,128)(2,1)S(1)}, bf16[2,4,1152]{2,1,0:T(4,128)(2,1)S(1)}, u32[]{:S(2)}, u32[]{:S(2)}) collective-permute-start(bf16[2,4,1152]{2,1,0:T(4,128)(2,1)S(1)} %get-tuple-element.412), channel_id=1, source_target_pairs={{2,0},{4,2},{6,4},{8,6},{10,8},{12,10},{14,12},{16,14},{18,16},{20... | collective-permute-start | bytes 55304 | tf_op jit(solution)/shard_map/ppermute | solution.py:35
  943.9 72.1 %slice-start.4 = ((s8[9437184]{0:T(1024)(128)(4,1)}), s8[4194304]{0:T(1024)(128)(4,1)S(1)}, s32[]{:S(2)}) async-start(s8[9437184]{0:T(1024)(128)(4,1)} %bitcast.730), calls=%async_computation.27 | async-start | bytes 8388608
  943.9 72.1 %slice-start.5 = ((s8[9437184]{0:T(1024)(128)(4,1)}), s8[4194304]{0:T(1024)(128)(4,1)S(1)}, s32[]{:S(2)}) async-start(s8[9437184]{0:T(1024)(128)(4,1)} %bitcast.730), calls=%async_computation.28 | async-start | bytes 8388608
  951.1 65.0 %slice-start.6 = ((s8[9437184]{0:T(1024)(128)(4,1)}), s8[1048576]{0:T(1024)(128)(4,1)S(1)}, s32[]{:S(2)}) async-start(s8[9437184]{0:T(1024)(128)(4,1)} %bitcast.730), calls=%async_computation.29 | async-start | bytes 2097152
  955.5 63.0 %copy-start.36 = (f32[2,1024,768]{2,1,0:T(8,128)}, f32[2,1024,768]{2,1,0:T(8,128)S(1)}, u32[]{:S(2)}) copy-start(f32[2,1024,768]{2,1,0:T(8,128)S(1)} %convert_add_fusion) | copy-start | bytes 18874372
  957.0 73.6 %collective-permute-start.7 = (bf16[2,512,768]{2,1,0:T(8,128)(2,1)}, bf16[2,512,768]{2,1,0:T(8,128)(2,1)}, u32[]{:S(2)}, u32[]{:S(2)}) collective-permute-start(bf16[2,512,768]{2,1,0:T(8,128)(2,1)} %slice.738), channel_id=1, source_target_pairs={{2,0},{4,2},{6,4},{8,6},{10,8},{12,10},{14,12},{16,14},{18,16},{20... | collective-permute-start | bytes 4718600 | tf_op jit(solution)/shard_map/ppermute | solution.py:16
  1019.8 11.9 collective-permute-start.9
  1445.5 48.8 %reduce-scatter.39.cloned.1.call-start = ((), (), s32[]{:S(2)}) async-start(), calls=%async_computation.21 | async-start | bytes 147456
  1446.4 52.0 %reduce-scatter.31.cloned.1.call-start = ((), (), s32[]{:S(2)}) async-start(), calls=%async_computation.17 | async-start | bytes 884736
  1448.5 68.4 %reduce-scatter.33.cloned.1.call-start = ((), (), s32[]{:S(2)}) async-start(), calls=%async_computation.18 | async-start | bytes 884736
  1449.7 85.3 %reduce-scatter.35.cloned.1.call-start = ((), (), s32[]{:S(2)}) async-start(), calls=%async_computation.19 | async-start | bytes 884736
  1450.8 101.9 %reduce-scatter.41.cloned.1.call-start = ((), (), s32[]{:S(2)}) async-start(), calls=%async_computation.22 | async-start | bytes 884736
  1451.9 118.2 %reduce-scatter.23.cloned.1.call-start = ((), (), s32[]{:S(2)}) async-start(), calls=%async_computation.13 | async-start | bytes 884736 | tf_op jit(solution)/shard_map/reduce_scatter | solution.py:487
  1452.5 142.3 %reduce-scatter.25.cloned.1.call-start = ((), (), s32[]{:S(2)}) async-start(), calls=%async_computation.14 | async-start | bytes 1769472 | tf_op jit(solution)/shard_map/reduce_scatter | solution.py:505
  1453.3 178.4 %reduce-scatter.29.cloned.1.call-start = ((), (), s32[]{:S(2)}) async-start(), calls=%async_computation.16 | async-start | bytes 3538944 | tf_op jit(solution)/shard_map/reduce_scatter | solution.py:523
  1453.8 215.5 %reduce-scatter.27.cloned.1.call-start = ((), (), s32[]{:S(2)}) async-start(), calls=%async_computation.15 | async-start | bytes 3538944 | tf_op jit(solution)/shard_map/reduce_scatter | solution.py:517
  (197 other events, 1208.0 us)
Sparse Core Ops, SparseCore 0:
  9.6 31.7 all-gather.11
  43.0 36.2 all-gather.13
  81.3 39.7 all-gather.15
  1445.6 22.6 reduce-scatter.36
  1470.4 9.9 reduce-scatter.38
  1483.1 15.2 reduce-scatter.30
  1501.3 15.5 reduce-scatter.32
  1519.8 15.2 reduce-scatter.34
  1537.4 15.2 reduce-scatter.40
  1554.8 15.2 reduce-scatter.22
  1573.0 21.7 reduce-scatter.24
  1596.9 34.7 reduce-scatter.28
  1634.6 34.6 reduce-scatter.26
where the time goes:
time: 1690 us; the launch traced here: 1680 us
  blocking collectives  507 us (30%)
  matrix products  355 us (21%)
  waiting for transfers between devices  307 us (18%)
  other arithmetic  216 us (13%)
  local copies, waits for them, and re-layouts  210 us (12%)
  starting transfers between devices  33.4 us (2%)
  loops' own time  30.2 us (2%)
  between operations  20.6 us (1%)
    psum x1, blocking collectives, on_device(): lax.psum((grad_query_w, grad_query_b, grad_key_w, grad_value_w, grad_valu...  404 us
    ppermute x8, waiting for transfers between devices, passed_along(): return lax.ppermute(shard, axis, pairs)  145 us
    dot_general x12, matrix products, pair_scores(): jnp.einsum('qhd,khd->hqk', query_pair, key_pair, preferred_element_type=j...  94.2 us
    unnamed x400, local copies, waits for them, and re-layouts  60.8 us
    dot_general x6, matrix products, attend_backward(): jnp.einsum('qhd,khd->hqk', grad_pair, value_pair, preferred_element_type=...  54.3 us
    unnamed x19, waiting for transfers between devices  54.2 us
    convert_element_type x6, other arithmetic, attend_backward(): grad_scores = (probs * (grad_probs - inner_sum)).astype(jnp.bfloat16)  49.4 us
    dynamic_update_slice x4, local copies, waits for them, and re-layouts, on_device(): lax.map(attend_backward, (query_blocks, window, own_seg, key_seg, grad_at...  43.4 us
  transfers between devices with their start and end apart: 25, of which 10 were waited for; matrix products, arithmetic and copies ran while one was open for 23% of the time, Pallas kernels for 0%

commit v1 on v0

v1 whole, which is shorter than its diff:
```python
import functools

import jax
import jax.numpy as jnp
from jax import lax
from jax.experimental import pallas as pl
from jax.experimental.pallas import tpu as pltpu
from jax.sharding import PartitionSpec as P

HEADS = 6
HEAD_DIM = 64
KERNEL = 9
GROUPS = 2
HOPS = 2


def passed_along(shard, axis, by):
    count = lax.axis_size(axis)
    pairs = [(i, i + by) for i in range(count) if 0 <= i + by < count]
    return lax.ppermute(shard, axis, pairs)


def for_sending(shard):

    def short(part):
        return part.astype(jnp.bfloat16) if part.dtype == jnp.float32 else part

    return jax.tree.map(short, shard)


def with_halo(block, sides, width):
    for axis, dim in sides:
        count = lax.axis_size(axis)
        forward = [(i, i + 1) for i in range(count - 1)]
        backward = [(target, source) for source, target in forward]
        low = lax.ppermute(
            lax.slice_in_dim(block, block.shape[dim] - width, None, axis=dim), axis, forward
        )
        high = lax.ppermute(lax.slice_in_dim(block, 0, width, axis=dim), axis, backward)
        block = jnp.concatenate([low, block, high], axis=dim)
    return block


def layer_norm(values, gain, shift):
    center = values - jnp.mean(values, axis=-1, keepdims=True)
    spread = jnp.mean(center * center, axis=-1, keepdims=True)
    return center * lax.rsqrt(spread + 1e-05) * gain + shift


def gelu_exact(values):
    return jax.nn.gelu(values, approximate=False)


def kernel_softmax(values):
    return jax.nn.softmax(values, axis=-1)


def product(left, right):
    return jnp.dot(left, right, preferred_element_type=jnp.float32)


def product_tn(left, right):
    return jnp.einsum("na,nb->ab", left, right, preferred_element_type=jnp.float32)


def product_nt(left, right):
    return jnp.einsum("na,ba->nb", left, right, preferred_element_type=jnp.float32)


def column_sum(values):
    return jnp.sum(values.astype(jnp.float32), axis=0)


def placed_rows(term, before, after):
    widths = [(0, 0)] * term.ndim
    widths[1] = (before, after)
    return jnp.pad(term, widths)


TILE = 256
NEG = -1000000000.0
LANES = 128
HEADS_HERE = HEADS // 2


def rows_nt(left, right):
    return lax.dot_general(
        left, right, (((1,), (1,)), ((), ())), preferred_element_type=jnp.float32
    )


def lane_half(block, upper):
    lane = lax.broadcasted_iota(jnp.int32, block.shape, 1)
    keep = lane >= HEAD_DIM if upper else lane < HEAD_DIM
    return jnp.where(keep, block, jnp.zeros_like(block))


def same_document(segk_ref, segq_ref, j):
    cols = pl.ds(pl.multiple_of(j * TILE, TILE), TILE)
    row = segk_ref[0:1, cols]
    column = jnp.broadcast_to(row, (LANES, TILE)).T
    wide = jnp.concatenate([column] * (TILE // LANES), axis=1)
    return wide == segq_ref[0:1, :]


def load_queries(q_ref, qm_ref):
    scale = jnp.asarray(HEAD_DIM ** (-0.5), q_ref.dtype)
    first = q_ref[:, 0:LANES] * scale
    qm_ref[0] = lane_half(first, False)
    qm_ref[1] = lane_half(first, True)
    qm_ref[2] = lane_half(q_ref[:, LANES : 2 * LANES] * scale, False)


KEY_GROUP = (0, 0, 1)
VALUE_GROUP = (2, 2, 1)


def lane_group(group):
    return slice(group * LANES, (group + 1) * LANES)


def attend_kernel(bounds, q_ref, kv_ref, segk_ref, segq_ref, out_ref, outt_ref, lse_ref,
                  qm_ref, m_ref, l_ref, acc_ref, low_ref):
    tile = pl.program_id(0)
    load_queries(q_ref, qm_ref)
    m_ref[...] = jnp.full_like(m_ref, -jnp.inf)
    l_ref[...] = jnp.zeros_like(l_ref)
    acc_ref[...] = jnp.zeros_like(acc_ref)
    low_ref[...] = jnp.zeros_like(low_ref)

    def step(j, carry):
        rows = pl.ds(pl.multiple_of(j * TILE, TILE), TILE)
        same = same_document(segk_ref, segq_ref, j)
        values_t = kv_ref[rows, LANES : 3 * LANES].T
        value_rows = (2 * HEAD_DIM, 3 * HEAD_DIM, HEAD_DIM)
        for head in range(HEADS_HERE):
            keys = kv_ref[rows, lane_group(KEY_GROUP[head])]
            scores = jnp.where(same, rows_nt(keys, qm_ref[head]), NEG)
            old = m_ref[head : head + 1, :]
            top = jnp.maximum(old, jnp.max(scores, axis=0, keepdims=True))
            expo = jnp.exp(scores - top)
            alpha = jnp.exp(old - top)
            m_ref[head : head + 1, :] = top
            l_ref[head : head + 1, :] = l_ref[head : head + 1, :] * alpha + jnp.sum(
                expo, axis=0, keepdims=True
            )
            high = expo.astype(jnp.bfloat16)
            rest = (expo - high.astype(jnp.float32)).astype(jnp.bfloat16)
            span = slice(head * HEAD_DIM, (head + 1) * HEAD_DIM)
            vals = values_t[value_rows[head] : value_rows[head] + HEAD_DIM, :]
            acc_ref[span, :] = acc_ref[span, :] * alpha + jnp.dot(
                vals, high, preferred_element_type=jnp.float32
            )
            low_ref[span, :] = low_ref[span, :] * alpha + jnp.dot(
                vals, rest, preferred_element_type=jnp.float32
            )
        return carry

    lax.fori_loop(bounds[0, tile], bounds[1, tile], step, 0)
    lse_ref[...] = m_ref[...] + jnp.log(l_ref[...])
    used = HEADS_HERE * HEAD_DIM
    for head in range(HEADS_HERE):
        span = slice(head * HEAD_DIM, (head + 1) * HEAD_DIM)
        inv = 1.0 / l_ref[head : head + 1, :]
        acc_ref[span, :] = acc_ref[span, :] * inv
        low_ref[span, :] = low_ref[span, :] * inv
    outt_ref[...] = acc_ref[...] + low_ref[...]
    out_ref[...] = acc_ref[...].T.astype(jnp.bfloat16)


def attend(bounds, queries, window, seg_keys, seg_queries):
    rows, wide = queries.shape
    span, width = window.shape
    return pl.pallas_call(
        attend_kernel,
        grid_spec=pltpu.PrefetchScalarGridSpec(
            num_scalar_prefetch=1,
            grid=(rows // TILE,),
            in_specs=[
                pl.BlockSpec((TILE, wide), lambda i, b: (i, 0)),
                pl.BlockSpec((span, width), lambda i, b: (0, 0)),
                pl.BlockSpec((8, span), lambda i, b: (0, 0)),
                pl.BlockSpec((8, TILE), lambda i, b: (0, i)),
            ],
            out_specs=[
                pl.BlockSpec((TILE, wide), lambda i, b: (i, 0)),
                pl.BlockSpec((wide, TILE), lambda i, b: (0, i)),
                pl.BlockSpec((8, TILE), lambda i, b: (0, i)),
            ],
            scratch_shapes=[
                pltpu.VMEM((HEADS_HERE, TILE, LANES), jnp.bfloat16),
                pltpu.VMEM((8, TILE), jnp.float32),
                pltpu.VMEM((8, TILE), jnp.float32),
                pltpu.VMEM((wide, TILE), jnp.float32),
                pltpu.VMEM((wide, TILE), jnp.float32),
            ],
        ),
        out_shape=[
            jax.ShapeDtypeStruct((rows, wide), jnp.bfloat16),
            jax.ShapeDtypeStruct((wide, rows), jnp.float32),
            jax.ShapeDtypeStruct((8, rows), jnp.float32),
        ],
        compiler_params=pltpu.CompilerParams(vmem_limit_bytes=40 * 2**20),
        name="attend",
    )(bounds, queries, window, seg_keys, seg_queries)


def attend_back_kernel(bounds, q_ref, kv_ref, segk_ref, segq_ref, grad_ref, outt_ref, lse_ref,
                       dq_ref, dkv_ref, qm_ref, gm_ref, delta_ref, dq_acc, dkv_acc):
    tile = pl.program_id(0)

    @pl.when(tile == 0)
    def _():
        dkv_acc[...] = jnp.zeros_like(dkv_acc)

    load_queries(q_ref, qm_ref)
    gm_ref[0] = lane_half(grad_ref[:, 0:LANES], False)
    gm_ref[1] = lane_half(grad_ref[:, 0:LANES], True)
    gm_ref[2] = lane_half(grad_ref[:, LANES : 2 * LANES], True)
    grads_t = grad_ref[...].astype(jnp.float32).T
    grad_rows = (0, HEAD_DIM, 3 * HEAD_DIM)
    for head in range(HEADS_HERE):
        span = slice(head * HEAD_DIM, (head + 1) * HEAD_DIM)
        delta_ref[head : head + 1, :] = jnp.sum(
            grads_t[grad_rows[head] : grad_rows[head] + HEAD_DIM, :] * outt_ref[span, :],
            axis=0, keepdims=True,
        )
    dq_acc[...] = jnp.zeros_like(dq_acc)

    def step(j, carry):
        rows = pl.ds(pl.multiple_of(j * TILE, TILE), TILE)
        same = same_document(segk_ref, segq_ref, j)
        keys_t = kv_ref[rows, 0 : 2 * LANES].T
        sums = [dkv_acc[rows, lane_group(g)] for g in range(3)]
        for head in range(HEADS_HERE):
            span = slice(head * HEAD_DIM, (head + 1) * HEAD_DIM)
            keys = kv_ref[rows, lane_group(KEY_GROUP[head])]
            vals = kv_ref[rows, lane_group(VALUE_GROUP[head])]
            scores = rows_nt(keys, qm_ref[head])
            probs = jnp.where(same, jnp.exp(scores - lse_ref[head : head + 1, :]), 0.0)
            dprobs = rows_nt(vals, gm_ref[head])
            dscores = (probs * (dprobs - delta_ref[head : head + 1, :])).astype(jnp.bfloat16)
            dq_acc[span, :] += jnp.dot(
                keys_t[span, :], dscores, preferred_element_type=jnp.float32
            )
            sums[KEY_GROUP[head]] += jnp.dot(
                dscores, qm_ref[head], preferred_element_type=jnp.float32
            )
            sums[VALUE_GROUP[head]] += jnp.dot(
                probs.astype(jnp.bfloat16), gm_ref[head], preferred_element_type=jnp.float32
            )
        for g in range(3):
            dkv_acc[rows, lane_group(g)] = sums[g]
        return carry

    lax.fori_loop(bounds[0, tile], bounds[1, tile], step, 0)
    dq_ref[...] = (dq_acc[...].T * HEAD_DIM ** (-0.5)).astype(dq_ref.dtype)

    @pl.when(tile == pl.num_programs(0) - 1)
    def _():
        dkv_ref[...] = dkv_acc[...].astype(dkv_ref.dtype)


def attend_back(bounds, queries, window, seg_keys, seg_queries, grads, outt, lse):
    rows, wide = queries.shape
    span, width = window.shape
    return pl.pallas_call(
        attend_back_kernel,
        grid_spec=pltpu.PrefetchScalarGridSpec(
            num_scalar_prefetch=1,
            grid=(rows // TILE,),
            in_specs=[
                pl.BlockSpec((TILE, wide), lambda i, b: (i, 0)),
                pl.BlockSpec((span, width), lambda i, b: (0, 0)),
                pl.BlockSpec((8, span), lambda i, b: (0, 0)),
                pl.BlockSpec((8, TILE), lambda i, b: (0, i)),
                pl.BlockSpec((TILE, wide), lambda i, b: (i, 0)),
                pl.BlockSpec((wide, TILE), lambda i, b: (0, i)),
                pl.BlockSpec((8, TILE), lambda i, b: (0, i)),
            ],
            out_specs=[
                pl.BlockSpec((TILE, wide), lambda i, b: (i, 0)),
                pl.BlockSpec((span, width), lambda i, b: (0, 0)),
            ],
            scratch_shapes=[
                pltpu.VMEM((HEADS_HERE, TILE, LANES), jnp.bfloat16),
                pltpu.VMEM((HEADS_HERE, TILE, LANES), jnp.bfloat16),
                pltpu.VMEM((8, TILE), jnp.float32),
                pltpu.VMEM((wide, TILE), jnp.float32),
                pltpu.VMEM((span, width), jnp.float32),
            ],
        ),
        out_shape=[
            jax.ShapeDtypeStruct((rows, wide), jnp.bfloat16),
            jax.ShapeDtypeStruct((span, width), jnp.bfloat16),
        ],
        compiler_params=pltpu.CompilerParams(vmem_limit_bytes=48 * 2**20),
        name="attend_back",
    )(bounds, queries, window, seg_keys, seg_queries, grads, outt, lse)


def rolled(part):
    return jnp.concatenate([part[..., HEAD_DIM:], part[..., :HEAD_DIM]], axis=-1)


def joined_halves(lower, upper):
    return jnp.concatenate([lower[..., :HEAD_DIM], upper[..., HEAD_DIM:]], axis=-1)


def lanes_of(values):
    return [values[..., lane_group(g)] for g in range(3)]


def parts_of_queries(queries, upper):
    one, two, three = lanes_of(queries)
    swapped = rolled(two)
    first, second = (swapped, two) if upper else (two, swapped)
    return jnp.stack(
        [jnp.concatenate([one, first], axis=-1), jnp.concatenate([three, second], axis=-1)], axis=1
    ).reshape(TEAM, queries.shape[1], 2 * LANES)


def parts_of_keys(keys, values):
    k = lanes_of(keys)
    v = lanes_of(values)
    low = jnp.concatenate([k[0], joined_halves(k[1], rolled(v[1])), v[0]], axis=-1)
    high = jnp.concatenate([k[2], joined_halves(rolled(k[1]), v[1]), v[2]], axis=-1)
    return jnp.stack([low, high], axis=1).reshape(TEAM, keys.shape[1], 3 * LANES)


def natural_rows(parts):
    pairs = parts.reshape(TEAM // 2, 2, parts.shape[1], 2 * LANES)
    low, high = pairs[:, 0], pairs[:, 1]
    middle = joined_halves(low[..., LANES:], rolled(high[..., LANES:]))
    return jnp.concatenate([low[..., :LANES], middle, high[..., :LANES]], axis=-1)


def natural_keys(parts):
    pairs = parts.reshape(TEAM // 2, 2, parts.shape[1], 3 * LANES)
    low, high = lanes_of(pairs[:, 0]), lanes_of(pairs[:, 1])
    keys = jnp.concatenate([low[0], joined_halves(low[1], rolled(high[1])), high[0]], axis=-1)
    values = jnp.concatenate([low[2], joined_halves(rolled(low[1]), high[1]), high[2]], axis=-1)
    return keys, values


TEAM = 4


def flip(index, step):
    return index + step * (1 - 2 * lax.rem(lax.div(index, step), 2))


def mate(rank, offset):
    if offset % 2:
        rank = flip(rank, 1)
    if offset // 2:
        rank = flip(rank, 2)
    return rank


def greet(peers):
    barrier = pltpu.get_barrier_semaphore()
    for peer in peers:
        pl.semaphore_signal(
            barrier, inc=1, device_id=peer, device_id_type=pl.DeviceIdType.MESH
        )
    pl.semaphore_wait(barrier, len(peers))


def remote(src, dst, send, recv, peer):
    return pltpu.make_async_remote_copy(
        src_ref=src,
        dst_ref=dst,
        send_sem=send,
        recv_sem=recv,
        device_id=peer,
        device_id_type=pl.DeviceIdType.MESH,
    )


def shard_view(ref, part, rows, count):
    if len(ref.shape) == 3:
        return ref.at[:, pl.ds(part * rows, count), :]
    return ref.at[pl.ds(part * rows, count), :]


def gather_kernel(count, *refs):
    shards, fulls = refs[:count], refs[count : 2 * count]
    send_y, recv_y, send_c, recv_c, local = refs[2 * count :]
    me, side = lax.axis_index("ctx"), lax.axis_index("wsh")
    core = lax.rem(me, 2)
    twin, across = {"ctx": flip(me, 1)}, {"wsh": 1 - side}
    greet([twin, across])
    copies = []

    def half(ref, base, rows):
        view = pl.ds(pl.multiple_of(base + core * (rows // 2), 16), rows // 2)
        return ref.at[:, view, :] if len(ref.shape) == 3 else ref.at[view, :]

    def whole(ref, base, rows):
        view = pl.ds(pl.multiple_of(base, 16), rows)
        return ref.at[:, view, :] if len(ref.shape) == 3 else ref.at[view, :]

    for i in range(count):
        rows = shards[i].shape[-2]
        copy = remote(
            half(shards[i], 0, rows), half(fulls[i], side * rows, rows),
            send_y.at[i], recv_y.at[i], across,
        )
        copy.start()
        copies.append(copy)
    own = []
    for i in range(count):
        rows = shards[i].shape[-2]
        copy = pltpu.make_async_copy(shards[i], whole(fulls[i], side * rows, rows), local.at[i])
        copy.start()
        own.append(copy)
    passed = []
    for i in range(count):
        rows = shards[i].shape[-2]
        copies[i].wait_recv()
        came = half(fulls[i], (1 - side) * rows, rows)
        copy = remote(came, came, send_c.at[i], recv_c.at[i], twin)
        copy.start()
        passed.append(copy)
    for i in range(count):
        copies[i].wait_send()
        own[i].wait()
        passed[i].wait()


def gather_weights(shards):
    count = len(shards)
    fulls = [
        jax.ShapeDtypeStruct(s.shape[:-2] + (2 * s.shape[-2], s.shape[-1]), s.dtype) for s in shards
    ]
    return pl.pallas_call(
        functools.partial(gather_kernel, count),
        out_shape=fulls,
        in_specs=[pl.BlockSpec(memory_space=pl.ANY)] * count,
        out_specs=[pl.BlockSpec(memory_space=pl.ANY)] * count,
        scratch_shapes=[pltpu.SemaphoreType.DMA((count,))] * 5,
        compiler_params=pltpu.CompilerParams(collective_id=0, has_side_effects=True),
        name="gather_weights",
    )(*shards)


def spread_kernel(kv_ref, q_ref, win_ref, out_ref, send_kv, recv_kv, send_q, recv_q,
                  send_l, recv_l, send_r, recv_r):
    me = lax.axis_index("ctx")
    count = lax.axis_size("ctx")
    rank = lax.rem(me, TEAM)
    base = me - rank
    team = lax.div(me, TEAM)
    teams = count // TEAM
    block = kv_ref.shape[1]
    halo = (TEAM - 1) * block
    right, left = lax.rem(me + TEAM, count), lax.rem(me + count - TEAM, count)
    greet([{"ctx": base + mate(rank, o)} for o in range(1, TEAM)] + [{"ctx": right}, {"ctx": left}])

    def place(r):
        return win_ref.at[pl.ds(pl.multiple_of(halo + r * block, 16), block), :]

    kv_copies, q_copies = [], []
    own_kv = pltpu.make_async_copy(kv_ref.at[rank], place(rank), recv_kv.at[0])
    own_kv.start()
    own_q = pltpu.make_async_copy(q_ref.at[rank], out_ref.at[rank], recv_q.at[0])
    own_q.start()
    for o in range(1, TEAM):
        other = mate(rank, o)
        copy = remote(kv_ref.at[other], place(rank), send_kv.at[o], recv_kv.at[o],
                      {"ctx": base + other})
        copy.start()
        kv_copies.append(copy)
    for o in range(1, TEAM):
        other = mate(rank, o)
        copy = remote(q_ref.at[other], out_ref.at[rank], send_q.at[o], recv_q.at[o],
                      {"ctx": base + other})
        copy.start()
        q_copies.append(copy)

    def onward(o):
        r = mate(rank, o)
        to_right = remote(
            place(r), win_ref.at[pl.ds(pl.multiple_of((r + TEAM - 1) % TEAM * block, 16), block), :],
            send_r.at[o], recv_r.at[o], {"ctx": right},
        )
        to_left = remote(
            place(r),
            win_ref.at[pl.ds(pl.multiple_of(halo + TEAM * block + lax.rem(r, TEAM - 1) * block, 16), block), :],
            send_l.at[o], recv_l.at[o], {"ctx": left},
        )
        return r, to_right, to_left

    for o in range(TEAM):
        if o == 0:
            own_kv.wait()
        else:
            kv_copies[o - 1].wait_recv()
        r, to_right, to_left = onward(o)
        pl.when((r >= 1) & (team < teams - 1))(to_right.start)
        pl.when((r <= TEAM - 2) & (team > 0))(to_left.start)
    own_q.wait()
    for copy in kv_copies:
        copy.wait_send()
    for copy in q_copies:
        copy.wait()
    for o in range(TEAM):
        r, to_right, to_left = onward(o)
        pl.when((r >= 1) & (team < teams - 1))(to_right.wait_send)
        pl.when((r <= TEAM - 2) & (team > 0))(to_left.wait_send)
        pl.when((r >= 1) & (team > 0))(to_right.wait_recv)
        pl.when((r <= TEAM - 2) & (team < teams - 1))(to_left.wait_recv)


def spread(kv_parts, q_parts):
    team, block, width = kv_parts.shape
    return pl.pallas_call(
        spread_kernel,
        out_shape=[
            jax.ShapeDtypeStruct(((3 * team - 2) * block, width), kv_parts.dtype),
            jax.ShapeDtypeStruct(q_parts.shape, q_parts.dtype),
        ],
        in_specs=[pl.BlockSpec(memory_space=pl.ANY)] * 2,
        out_specs=[pl.BlockSpec(memory_space=pl.ANY)] * 2,
        scratch_shapes=[pltpu.SemaphoreType.DMA((team,))] * 8,
        compiler_params=pltpu.CompilerParams(collective_id=1, has_side_effects=True),
        name="spread",
    )(kv_parts, q_parts)


def swap_kernel(src_ref, out_ref, send, recv):
    me = lax.axis_index("ctx")
    rank = lax.rem(me, TEAM)
    base = me - rank
    greet([{"ctx": base + mate(rank, o)} for o in range(1, TEAM)])
    copies = [pltpu.make_async_copy(src_ref.at[rank], out_ref.at[rank], recv.at[0])]
    for o in range(1, TEAM):
        other = mate(rank, o)
        copies.append(
            remote(src_ref.at[other], out_ref.at[rank], send.at[o], recv.at[o],
                   {"ctx": base + other})
        )
    for copy in copies:
        copy.start()
    for copy in copies:
        copy.wait()


def swap(parts, ident):
    return pl.pallas_call(
        swap_kernel,
        out_shape=jax.ShapeDtypeStruct(parts.shape, parts.dtype),
        in_specs=[pl.BlockSpec(memory_space=pl.ANY)],
        out_specs=pl.BlockSpec(memory_space=pl.ANY),
        scratch_shapes=[pltpu.SemaphoreType.DMA((TEAM,))] * 2,
        compiler_params=pltpu.CompilerParams(collective_id=ident, has_side_effects=True),
        name="swap",
    )(parts)


def collect_kernel(win_ref, dq_ref, kv_out, q_out, from_right, from_left, mine, total,
                   send_q, recv_q, send_z, recv_z, load, send_kv, recv_kv):
    me = lax.axis_index("ctx")
    count = lax.axis_size("ctx")
    rank = lax.rem(me, TEAM)
    base = me - rank
    team = lax.div(me, TEAM)
    teams = count // TEAM
    block = dq_ref.shape[1]
    halo = (TEAM - 1) * block
    right, left = lax.rem(me + TEAM, count), lax.rem(me + count - TEAM, count)
    greet([{"ctx": base + mate(rank, o)} for o in range(1, TEAM)] + [{"ctx": right}, {"ctx": left}])
    to_left = remote(win_ref.at[pl.ds(0, halo), :], from_right, send_z.at[0], recv_z.at[0],
                     {"ctx": left})
    to_right = remote(win_ref.at[pl.ds(halo + TEAM * block, halo), :], from_left, send_z.at[1],
                      recv_z.at[1], {"ctx": right})
    pl.when(team > 0)(to_left.start)
    pl.when(team < teams - 1)(to_right.start)
    center = pltpu.make_async_copy(win_ref.at[pl.ds(halo, TEAM * block), :], mine, load.at[0])
    center.start()
    own_q = pltpu.make_async_copy(dq_ref.at[rank], q_out.at[rank], recv_q.at[0])
    own_q.start()
    q_copies = []
    for o in range(1, TEAM):
        other = mate(rank, o)
        copy = remote(dq_ref.at[other], q_out.at[rank], send_q.at[o], recv_q.at[o],
                      {"ctx": base + other})
        copy.start()
        q_copies.append(copy)

    @pl.when(team == 0)
    def _():
        from_left[...] = jnp.zeros_like(from_left)

    @pl.when(team == teams - 1)
    def _():
        from_right[...] = jnp.zeros_like(from_right)

    center.wait()
    pl.when(team < teams - 1)(to_left.wait_recv)
    pl.when(team > 0)(to_right.wait_recv)
    for r in range(TEAM):
        rows = pl.ds(r * block, block)
        value = mine[rows, :].astype(jnp.float32)
        if r < TEAM - 1:
            value += from_left[rows, :].astype(jnp.float32)
        if r > 0:
            value += from_right[pl.ds((r - 1) * block, block), :].astype(jnp.float32)
        total[r] = value.astype(total.dtype)
    kv_copies = [pltpu.make_async_copy(total.at[rank], kv_out.at[rank], recv_kv.at[0])]
    for o in range(1, TEAM):
        other = mate(rank, o)
        kv_copies.append(
            remote(total.at[other], kv_out.at[rank], send_kv.at[o], recv_kv.at[o],
                   {"ctx": base + other})
        )
    for copy in kv_copies:
        copy.start()
    own_q.wait()
    for copy in q_copies + kv_copies:
        copy.wait()
    pl.when(team > 0)(to_left.wait_send)
    pl.when(team < teams - 1)(to_right.wait_send)


def collect(window, dq_parts):
    team, block, _ = dq_parts.shape
    width = window.shape[1]
    halo = (team - 1) * block
    return pl.pallas_call(
        collect_kernel,
        out_shape=[
            jax.ShapeDtypeStruct((team, block, width), window.dtype),
            jax.ShapeDtypeStruct(dq_parts.shape, dq_parts.dtype),
        ],
        in_specs=[pl.BlockSpec(memory_space=pl.ANY)] * 2,
        out_specs=[pl.BlockSpec(memory_space=pl.ANY)] * 2,
        scratch_shapes=[
            pltpu.VMEM((halo, width), window.dtype),
            pltpu.VMEM((halo, width), window.dtype),
            pltpu.VMEM((team * block, width), window.dtype),
            pltpu.VMEM((team, block, width), window.dtype),
            pltpu.SemaphoreType.DMA((team,)),
            pltpu.SemaphoreType.DMA((team,)),
            pltpu.SemaphoreType.DMA((2,)),
            pltpu.SemaphoreType.DMA((2,)),
            pltpu.SemaphoreType.DMA((1,)),
            pltpu.SemaphoreType.DMA((team,)),
            pltpu.SemaphoreType.DMA((team,)),
        ],
        compiler_params=pltpu.CompilerParams(
            collective_id=4, has_side_effects=True, vmem_limit_bytes=32 * 2**20
        ),
        name="collect",
    )(window, dq_parts)


def reduce_kernel(levels, g_ref, out_ref, acc, mine, came, *rest):
    steps = len(levels)
    sends, recvs = rest[:steps], rest[steps : 2 * steps]
    load, send_sem, recv_sem, send_back, recv_back = rest[2 * steps :]
    me, side = lax.axis_index("ctx"), lax.axis_index("wsh")
    core = lax.rem(me, 2)
    twin, across = {"ctx": flip(me, 1)}, {"wsh": 1 - side}
    peers = [twin, across] + [{"ctx": flip(me, step)} for step in levels[1:]]
    greet(peers)
    rows = g_ref.shape[1]
    half = rows // 2

    def add(n, write):
        chunk = max(c for c in range(16, 385, 16) if n % c == 0)

        def body(i, carry):
            write(pl.ds(pl.multiple_of(i * chunk, 16), chunk))
            return carry

        lax.fori_loop(0, n // chunk, body, 0)

    first = remote(
        g_ref.at[:, pl.ds(pl.multiple_of((1 - core) * half, 16), half), :], came,
        send_sem.at[0], recv_sem.at[0], twin,
    )
    first.start()
    own = pltpu.make_async_copy(
        g_ref.at[:, pl.ds(pl.multiple_of(core * half, 16), half), :], mine, load.at[0]
    )
    own.start()
    own.wait()
    first.wait()

    def level0(view):
        sends[0][view, :] = (
            mine[1 - side, view, :].astype(jnp.float32) + came[1 - side, view, :].astype(jnp.float32)
        ).astype(jnp.bfloat16)
        acc[view, :] = mine[side, view, :].astype(jnp.float32) + came[side, view, :].astype(
            jnp.float32
        )

    add(half, level0)
    copy = remote(sends[0], recvs[0], send_sem.at[1], recv_sem.at[1], across)
    copy.start()
    copy.wait()
    start = jnp.int32(0)
    size = half
    arrived = recvs[0]
    for i, step in enumerate(levels[1:]):
        bit = lax.rem(lax.div(me, step), 2)
        size = size // 2
        keep = start + bit * size
        give = start + (1 - bit) * size
        shift_keep, shift_give = bit * size, (1 - bit) * size

        def both(view, arrived=arrived, keep=keep, give=give, sk=shift_keep, sg=shift_give, i=i):
            lo = view.start
            n = view.size
            g_rows = pl.ds(pl.multiple_of(give + lo, 16), n)
            k_rows = pl.ds(pl.multiple_of(keep + lo, 16), n)
            sends[i + 1][view, :] = (
                acc[g_rows, :]
                + arrived[pl.ds(pl.multiple_of(sg + lo, 16), n), :].astype(jnp.float32)
            ).astype(jnp.bfloat16)
            acc[k_rows, :] = acc[k_rows, :] + arrived[
                pl.ds(pl.multiple_of(sk + lo, 16), n), :
            ].astype(jnp.float32)

        add(size, both)
        copy = remote(
            sends[i + 1], recvs[i + 1], send_sem.at[i + 2], recv_sem.at[i + 2],
            {"ctx": flip(me, step)},
        )
        copy.start()
        copy.wait()
        arrived = recvs[i + 1]
        start = keep
    final = mine.at[0]

    def last(view):
        rows_ = pl.ds(pl.multiple_of(start + view.start, 16), view.size)
        mine[0, rows_, :] = (acc[rows_, :] + arrived[view, :].astype(jnp.float32)).astype(
            jnp.bfloat16
        )

    add(size, last)
    for i, step in reversed(list(enumerate(levels[1:]))):
        view = mine.at[0, pl.ds(pl.multiple_of(start, 16), size), :]
        copy = remote(view, view, send_back.at[i + 1], recv_back.at[i + 1], {"ctx": flip(me, step)})
        copy.start()
        copy.wait()
        start = start - lax.rem(lax.div(me, step), 2) * size
        size = size * 2
    here = out_ref.at[pl.ds(pl.multiple_of(core * half, 16), half), :]
    own = pltpu.make_async_copy(final, here, load.at[0])
    own.start()
    copy = remote(final, here, send_back.at[0], recv_back.at[0], twin)
    copy.start()
    own.wait()
    copy.wait()


def reduce_grads(packed):
    _, rows, width = packed.shape
    half = rows // 2
    levels, step = [1], 2
    while step < lax.axis_size("ctx"):
        levels.append(step)
        step *= 2
    sizes = [half >> i for i in range(len(levels))]
    return pl.pallas_call(
        functools.partial(reduce_kernel, tuple(levels)),
        out_shape=jax.ShapeDtypeStruct((rows, width), packed.dtype),
        in_specs=[pl.BlockSpec(memory_space=pl.ANY)],
        out_specs=pl.BlockSpec(memory_space=pl.ANY),
        scratch_shapes=[
            pltpu.VMEM((half, width), jnp.float32),
            pltpu.VMEM((2, half, width), jnp.bfloat16),
            pltpu.VMEM((2, half, width), jnp.bfloat16),
        ]
        + [pltpu.VMEM((n, width), jnp.bfloat16) for n in sizes] * 2
        + [
            pltpu.SemaphoreType.DMA((1,)),
            pltpu.SemaphoreType.DMA((len(levels) + 1,)),
            pltpu.SemaphoreType.DMA((len(levels) + 1,)),
            pltpu.SemaphoreType.DMA((len(levels),)),
            pltpu.SemaphoreType.DMA((len(levels),)),
        ],
        compiler_params=pltpu.CompilerParams(
            collective_id=5, has_side_effects=True, vmem_limit_bytes=56 * 2**20
        ),
        name="reduce_grads",
    )(packed)


def small_rows(vectors, depth, kernel_w, count):
    flat = jnp.concatenate([v.reshape(-1) for v in vectors])
    flat = jnp.pad(flat, (0, -flat.shape[0] % 384))
    rows = jnp.concatenate([depth, flat.reshape(-1, 384), kernel_w.T.reshape(-1, 384)])
    return jnp.pad(rows, ((0, count - rows.shape[0]), (0, 0)))


def on_device(
    hidden_in,
    segment_ids,
    out_grad,
    query_w,
    query_b,
    key_w,
    value_w,
    value_b,
    depth_kernel,
    point_w,
    point_b,
    kernel_w,
    kernel_b,
    conv_w,
    conv_b,
    output_w,
    output_b,
    norm1_gain,
    norm1_bias,
    inner_w,
    inner_b,
    outer_w,
    outer_b,
    norm2_gain,
    norm2_bias,
):
    vectors = [query_b, value_b, point_b, conv_b, output_b, norm1_gain, norm1_bias, inner_b,
               outer_b, norm2_gain, norm2_bias, kernel_b]
    small = small_rows(vectors, depth_kernel, kernel_w, 64)
    (key_mat, value_mat, query_mat, point_mat, conv_mat, small_full, output_mat, inner_mat,
     outer_mat) = gather_weights(
        [key_w, value_w, query_w, point_w, conv_w, small, output_w, inner_w, outer_w]
    )
    small_full = small_full.reshape(2, 64, 384)
    depth_taps = small_full[:, :KERNEL].transpose(1, 0, 2).reshape(KERNEL, -1)
    sizes = [v.shape[0] for v in vectors]
    total = sum(sizes)
    flat_rows_ = (total + 383) // 384
    flat = small_full[:, KERNEL : KERNEL + flat_rows_].reshape(2, -1)
    offsets = [sum(sizes[:i]) for i in range(len(sizes) + 1)]
    (query_vec, value_vec, point_vec, conv_vec, output_vec, gain_one, shift_one, inner_vec,
     outer_vec, gain_two, shift_two, kernel_vec) = [
        flat[:, offsets[i] : offsets[i + 1]].reshape(-1) for i in range(len(sizes))
    ]
    kernel_rows = kernel_w.shape[0] * kernel_w.shape[1] // 384
    kernel_mat = (
        small_full[:, KERNEL + flat_rows_ : KERNEL + flat_rows_ + kernel_rows]
        .reshape(2, kernel_w.shape[1], kernel_w.shape[0])
        .transpose(0, 2, 1)
        .reshape(-1, kernel_w.shape[1])
    )
    micro_count, seq_local, block_len, model_width = hidden_in.shape
    seq_count = micro_count * seq_local
    row_count = seq_count * block_len
    att_width = query_mat.shape[1]
    half_taps = KERNEL // 2
    flat_rows = hidden_in.reshape(row_count, model_width)
    position = lax.axis_index("ctx")
    seg_rows = segment_ids.reshape(seq_count, segment_ids.shape[2])
    pad_rows = (TEAM - 1) * block_len
    seg_pad = jnp.pad(seg_rows, ((0, 0), (pad_rows, pad_rows)), constant_values=-1)
    own_seg = lax.dynamic_slice_in_dim(seg_pad, position * block_len + pad_rows, block_len, 1)
    rank = lax.rem(position, TEAM)
    team_seg = lax.dynamic_slice(
        jnp.concatenate(
            [seg_pad[:, : pad_rows + seg_rows.shape[1]],
             jnp.full((seq_count, pad_rows), 2**24, seg_pad.dtype)], axis=1
        ),
        (lax.div(rank, 2), (position - rank) * block_len),
        (1, (3 * TEAM - 2) * block_len),
    )
    query_seg = team_seg[:, pad_rows : pad_rows + TEAM * block_len]
    lows = query_seg[0, ::TILE]
    highs = query_seg[0, TILE - 1 :: TILE]
    before = jnp.sum(team_seg < lows[:, None], axis=1, dtype=jnp.int32)
    through = jnp.sum(team_seg <= highs[:, None], axis=1, dtype=jnp.int32)
    bounds = jnp.stack([before // TILE, (through + TILE - 1) // TILE])
    seg_keys = jnp.broadcast_to(team_seg.astype(jnp.float32), (8, team_seg.shape[1]))
    seg_queries = jnp.broadcast_to(query_seg.astype(jnp.float32), (8, query_seg.shape[1]))
    rim_seg = lax.dynamic_slice_in_dim(
        seg_pad, position * block_len + pad_rows - half_taps, block_len + 2 * half_taps, 1
    )
    tap_mask = jnp.stack(
        [rim_seg[:, offset : offset + block_len] == own_seg for offset in range(KERNEL)], axis=2
    ).astype(jnp.float32)
    rimmed = with_halo(
        hidden_in.reshape(seq_count, block_len, model_width), (("ctx", 1),), half_taps
    )
    queries = (product(flat_rows, query_mat) + query_vec).astype(jnp.bfloat16)
    query_blocks = queries.reshape(seq_count, block_len, att_width)
    keys = product(flat_rows, key_mat).astype(jnp.bfloat16)
    values = (product(flat_rows, value_mat) + value_vec).astype(jnp.bfloat16)
    window, query_team = spread(
        parts_of_keys(
            keys.reshape(seq_count, block_len, att_width),
            values.reshape(seq_count, block_len, att_width),
        ),
        parts_of_queries(query_blocks, False),
    )
    query_team = query_team.reshape(TEAM * block_len, 2 * LANES)
    depth_sum = sum(
        (
            depth_taps[offset].astype(jnp.float32)
            * rimmed[:, offset : offset + block_len]
            * tap_mask[:, :, offset : offset + 1]
            for offset in range(KERNEL)
        )
    )
    depth_low = depth_sum.astype(jnp.bfloat16).reshape(row_count, model_width)
    span_keys = product(depth_low, point_mat) + point_vec
    mixed_low = (span_keys * queries).astype(jnp.bfloat16)
    logits = (product(mixed_low, kernel_mat) + kernel_vec).reshape(
        seq_count, block_len, HEADS, KERNEL
    )
    kernels, kern_pull = jax.vjp(kernel_softmax, logits)
    conv_ext = (product(rimmed.reshape(-1, model_width), conv_mat) + conv_vec).reshape(
        seq_count, block_len + 2 * half_taps, HEADS, HEAD_DIM
    )
    convolved = sum(
        (
            (kernels[..., offset] * tap_mask[:, :, offset : offset + 1])[..., None]
            * conv_ext[:, offset : offset + block_len]
            for offset in range(KERNEL)
        )
    )
    attended_team, attended_t, log_sums = attend(
        bounds, query_team, window, seg_keys, seg_queries
    )
    attended = natural_rows(swap(attended_team.reshape(TEAM, block_len, -1), 2))
    joined = jnp.concatenate(
        [
            attended.reshape(row_count, att_width),
            convolved.reshape(row_count, att_width).astype(jnp.bfloat16),
        ],
        axis=1,
    )
    branch = product(joined, output_mat) + output_vec
    normed, norm1_pull = jax.vjp(
        layer_norm, branch + flat_rows, gain_one.astype(jnp.float32), shift_one.astype(jnp.float32)
    )
    normed_low = normed.astype(jnp.bfloat16).reshape(row_count, GROUPS, -1)
    inner_pre = jnp.einsum(
        "ngd,gdf->ngf", normed_low, inner_mat, preferred_element_type=jnp.float32
    ) + inner_vec.reshape(GROUPS, -1)
    active, gelu_pull = jax.vjp(gelu_exact, inner_pre)
    active_low = active.astype(jnp.bfloat16)
    outer_out = (
        jnp.einsum("ngf,gfd->ngd", active_low, outer_mat, preferred_element_type=jnp.float32)
        + outer_vec.reshape(GROUPS, -1)
    ).reshape(row_count, model_width)
    final_out, norm2_pull = jax.vjp(
        layer_norm, outer_out + normed, gain_two.astype(jnp.float32), shift_two.astype(jnp.float32)
    )
    output = final_out.astype(jnp.bfloat16).reshape(hidden_in.shape)
    grad_sum2, grad_gain2, grad_shift2 = norm2_pull(
        out_grad.reshape(row_count, model_width).astype(jnp.float32)
    )
    grad_outer = grad_sum2.astype(jnp.bfloat16).reshape(row_count, GROUPS, -1)
    grad_outer_w = jnp.einsum(
        "ngf,ngd->gfd", active_low, grad_outer, preferred_element_type=jnp.float32
    )
    grad_outer_b = column_sum(grad_outer).reshape(-1)
    (grad_inner,) = gelu_pull(
        jnp.einsum("ngd,gfd->ngf", grad_outer, outer_mat, preferred_element_type=jnp.float32)
    )
    grad_inner = grad_inner.astype(jnp.bfloat16)
    grad_inner_w = jnp.einsum(
        "ngd,ngf->gdf", normed_low, grad_inner, preferred_element_type=jnp.float32
    )
    grad_inner_b = column_sum(grad_inner).reshape(-1)
    grad_normed = grad_sum2 + jnp.einsum(
        "ngf,gdf->ngd", grad_inner, inner_mat, preferred_element_type=jnp.float32
    ).reshape(row_count, model_width)
    grad_sum1, grad_gain1, grad_shift1 = norm1_pull(grad_normed)
    grad_branch = grad_sum1.astype(jnp.bfloat16)
    grad_output_w = product_tn(joined, grad_branch)
    grad_output_b = column_sum(grad_branch)
    grad_joined = product_nt(grad_branch, output_mat).astype(jnp.bfloat16)
    grad_attended = grad_joined[:, :att_width].reshape(seq_count, block_len, att_width)
    grad_conv = (
        grad_joined[:, att_width:]
        .astype(jnp.float32)
        .reshape(seq_count, block_len, HEADS, HEAD_DIM)
    )
    grad_kern_list = []
    ext_terms = []
    for offset in range(KERNEL):
        tap_weight = tap_mask[:, :, offset : offset + 1]
        grad_kern_list.append(
            jnp.sum(grad_conv * conv_ext[:, offset : offset + block_len], axis=-1) * tap_weight
        )
        ext_terms.append(
            placed_rows(
                (kernels[..., offset] * tap_weight)[..., None] * grad_conv,
                offset,
                2 * half_taps - offset,
            )
        )
    grad_ext = sum(ext_terms)
    (grad_logits,) = kern_pull(jnp.stack(grad_kern_list, axis=-1))
    grad_logits = grad_logits.reshape(row_count, HEADS * KERNEL).astype(jnp.bfloat16)
    grad_kernel_w = product_tn(mixed_low, grad_logits)
    grad_kernel_b = column_sum(grad_logits)
    grad_mixed = product_nt(grad_logits, kernel_mat)
    grad_spans = (grad_mixed * queries).astype(jnp.bfloat16)
    grad_query_conv = grad_mixed * span_keys
    grad_point_w = product_tn(depth_low, grad_spans)
    grad_point_b = column_sum(grad_spans)
    grad_depth = product_nt(grad_spans, point_mat).reshape(seq_count, block_len, model_width)
    grad_taps = []
    rim_terms = []
    for offset in range(KERNEL):
        masked_grad = grad_depth * tap_mask[:, :, offset : offset + 1]
        grad_taps.append(jnp.sum(masked_grad * rimmed[:, offset : offset + block_len], axis=(0, 1)))
        rim_terms.append(
            placed_rows(
                masked_grad * depth_taps[offset].astype(jnp.float32), offset, 2 * half_taps - offset
            )
        )
    grad_rim = sum(rim_terms)
    grad_depth_taps = jnp.stack(grad_taps, axis=0)
    rim_parts = jnp.concatenate([grad_ext.reshape(seq_count, -1, att_width), grad_rim], axis=2)
    edges = jnp.concatenate(
        [rim_parts[:, :half_taps], rim_parts[:, block_len + half_taps :]], axis=1
    )
    arrived = with_halo(edges.astype(jnp.bfloat16), (("ctx", 1),), half_taps).astype(edges.dtype)
    own_parts = (
        rim_parts[:, half_taps : half_taps + block_len]
        + placed_rows(arrived[:, :half_taps], 0, block_len - half_taps)
        + placed_rows(arrived[:, 3 * half_taps :], block_len - half_taps, 0)
    )
    grad_conv_vals = own_parts[..., :att_width].reshape(row_count, att_width).astype(jnp.bfloat16)
    grad_conv_w = product_tn(flat_rows, grad_conv_vals)
    grad_conv_b = column_sum(grad_conv_vals)
    grad_team = swap(parts_of_queries(grad_attended, True), 3).reshape(TEAM * block_len, 2 * LANES)
    grad_query_team, grad_window = attend_back(
        bounds, query_team, window, seg_keys, seg_queries, grad_team, attended_t, log_sums
    )
    kv_parts, dq_parts = collect(grad_window, grad_query_team.reshape(TEAM, block_len, -1))
    grad_query_att = natural_rows(dq_parts).astype(jnp.float32)
    grad_keys, grad_values = [
        part.reshape(row_count, att_width) for part in natural_keys(kv_parts)
    ]
    grad_queries = (grad_query_att.reshape(row_count, att_width) + grad_query_conv).astype(
        jnp.bfloat16
    )
    grad_query_w = product_tn(flat_rows, grad_queries)
    grad_query_b = column_sum(grad_queries)
    grad_key_w = product_tn(flat_rows, grad_keys)
    grad_value_w = product_tn(flat_rows, grad_values)
    grad_value_b = column_sum(grad_values)
    grad_input = (
        grad_sum1
        + product_nt(grad_queries, query_mat)
        + product_nt(grad_keys, key_mat)
        + product_nt(grad_values, value_mat)
        + product_nt(grad_conv_vals, conv_mat)
        + own_parts[..., att_width:].reshape(row_count, model_width)
    ).reshape(hidden_in.shape)
    low = lambda part: part.astype(jnp.bfloat16)
    halves = []
    for w in range(2):
        def cut(part, axis=0):
            size = part.shape[axis] // 2
            return lax.slice_in_dim(part, w * size, (w + 1) * size, axis=axis)

        grads = [cut(v) for v in (
            grad_query_b, grad_value_b, grad_point_b, grad_conv_b, grad_output_b, grad_gain1,
            grad_shift1, grad_inner_b, grad_outer_b, grad_gain2, grad_shift2, grad_kernel_b)]
        pieces = [cut(m) for m in (grad_key_w, grad_value_w, grad_query_w, grad_point_w, grad_conv_w)]
        pieces.append(small_rows(grads, cut(grad_depth_taps, 1), cut(grad_kernel_w), 64))
        pieces.append(cut(grad_output_w).reshape(-1, 384))
        pieces.append(cut(grad_inner_w, 1).reshape(-1, 384))
        pieces.append(cut(grad_outer_w, 1).reshape(-1, 384))
        halves.append(jnp.concatenate([low(p) for p in pieces]))
    packed = jnp.stack(halves)
    unit = 16 * lax.axis_size("ctx")
    packed = jnp.pad(packed, ((0, 0), (0, -packed.shape[1] % unit), (0, 0)))
    shared = reduce_grads(packed).astype(jnp.float32)
    taken = [0]

    def take(shape):
        rows = 1
        for n in shape:
            rows *= n
        rows //= 384
        taken[0] += rows
        return shared[taken[0] - rows : taken[0]].reshape(shape)

    o_key, o_value, o_query, o_point, o_conv = [take(key_w.shape) for _ in range(5)]
    o_small = take((64, 384))
    o_output = take(output_w.shape)
    o_inner = take(inner_w.shape)
    o_outer = take(outer_w.shape)
    flat = o_small[KERNEL : KERNEL + flat_rows_].reshape(-1)
    (o_query_b, o_value_b, o_point_b, o_conv_b, o_output_b, o_gain1, o_shift1, o_inner_b,
     o_outer_b, o_gain2, o_shift2, o_kernel_b) = [
        flat[offsets[i] : offsets[i + 1]] for i in range(len(sizes))
    ]
    o_kernel = (
        o_small[KERNEL + flat_rows_ : KERNEL + flat_rows_ + kernel_rows]
        .reshape(kernel_w.shape[1], kernel_w.shape[0])
        .T
    )
    shares = (
        o_query, o_query_b, o_key, o_value, o_value_b, o_small[:KERNEL], o_point, o_point_b,
        o_kernel, o_kernel_b, o_conv, o_conv_b, o_output, o_output_b, o_gain1, o_shift1,
        o_inner, o_inner_b, o_outer, o_outer_b, o_gain2, o_shift2,
    )
    return (output, grad_input) + shares


def solution(mesh):
    in_specs = (
        P(None, "wsh", "ctx", None),
        P(None, "wsh", None),
        P(None, "wsh", "ctx", None),
        P("wsh", None),
        P("wsh"),
        P("wsh", None),
        P("wsh", None),
        P("wsh"),
        P(None, "wsh"),
        P("wsh", None),
        P("wsh"),
        P("wsh", None),
        P("wsh"),
        P("wsh", None),
        P("wsh"),
        P("wsh", None),
        P("wsh"),
        P("wsh"),
        P("wsh"),
        P(None, "wsh", None),
        P("wsh"),
        P(None, "wsh", None),
        P("wsh"),
        P("wsh"),
        P("wsh"),
    )
    out_specs = (
        P(None, "wsh", "ctx", None),
        P(None, "wsh", "ctx", None),
        P("wsh", None),
        P("wsh"),
        P("wsh", None),
        P("wsh", None),
        P("wsh"),
        P(None, "wsh"),
        P("wsh", None),
        P("wsh"),
        P("wsh", None),
        P("wsh"),
        P("wsh", None),
        P("wsh"),
        P("wsh", None),
        P("wsh"),
        P("wsh"),
        P("wsh"),
        P(None, "wsh", None),
        P("wsh"),
        P(None, "wsh", None),
        P("wsh"),
        P("wsh"),
        P("wsh"),
    )
    return jax.shard_map(
        on_device, mesh=mesh, in_specs=in_specs, out_specs=out_specs, check_vma=False
    )
```

time: 1690 us -> 1010 us (0.60)
  Pallas kernels: 0 us -> 542 us
  blocking collectives: 507 us -> 0 us
  waiting for transfers between devices: 307 us -> 0.01 us
  matrix products: 355 us -> 123 us
  other arithmetic: 216 us -> 156 us
  local copies, waits for them, and re-layouts: 210 us -> 171 us
  loops' own time: 30.2 us -> 0 us
  starting transfers between devices: 33.4 us -> 9.14 us
    pallas_call x0 -> x8, Pallas kernels: none -> 542 us  [the longest x1 172 us: reduce_grads(): pl.pallas_call(functools.partial(reduce_kernel, tuple(levels)), out_shape...]
    psum x1 -> x0, blocking collectives: 404 us -> none  [on_device(): lax.psum((grad_query_w, grad_query_b, grad_key_w, grad_value_w, grad_valu...]
    dot_general x42 -> x0, matrix products: 237 us -> none  [the longest x12 94.2 us: pair_scores(): jnp.einsum('qhd,khd->hqk', query_pair, key_pair, preferred_element_type=j...]
    ppermute x8 -> x0, waiting for transfers between devices: 145 us -> none  [passed_along(): return lax.ppermute(shard, axis, pairs)]
    reduce_scatter x4 -> x0, waiting for transfers between devices: 108 us -> none  [the longest x1 34.8 us: on_device(): lax.psum_scatter(summed[16].astype(jnp.bfloat16), 'wsh', scatter_dimensio...]
    all_gather x14 -> x0, blocking collectives: 88.9 us -> none  [the longest x1 16.4 us: on_device(): lax.all_gather(value_w, 'wsh', axis=0, tiled=True)]
    unnamed x19 -> x0, waiting for transfers between devices: 54.2 us -> none
    dynamic_update_slice x12 -> x0, local copies, waits for them, and re-layouts: 44.6 us -> none  [the longest x4 43.4 us: on_device(): lax.map(attend_backward, (query_blocks, window, own_seg, key_seg, grad_at...]
  transfers between devices with their start and end apart: 25 -> 4, of which waited for: 10 -> 0; matrix products, arithmetic and copies ran while one was open for 23% -> 11% of each run, Pallas kernels for 0% -> 23%
where the time goes in v1:
time: 1010 us
  Pallas kernels  542 us (54%)
  local copies, waits for them, and re-layouts  171 us (17%)
  other arithmetic  156 us (15%)
  matrix products  123 us (12%)
    pallas_call x1, Pallas kernels, reduce_grads(): pl.pallas_call(functools.partial(reduce_kernel, tuple(levels)), out_shape...  172 us
    pallas_call x1, Pallas kernels, gather_weights(): pl.pallas_call(functools.partial(gather_kernel, count), out_shape=fulls,...  140 us
    pallas_call x1, Pallas kernels, collect(): pl.pallas_call(collect_kernel, out_shape=[jax.ShapeDtypeStruct((team, blo...  74.3 us
    pallas_call x1, Pallas kernels, attend_back(): pl.pallas_call(attend_back_kernel, grid_spec=pltpu.PrefetchScalarGridSpec...  51.7 us
    unnamed x457, local copies, waits for them, and re-layouts  50.7 us
    pallas_call x1, Pallas kernels, spread(): pl.pallas_call(spread_kernel, out_shape=[jax.ShapeDtypeStruct(((3 * team...  44.6 us
    dot_general x1, matrix products, on_device(): jnp.einsum('ngd,gdf->ngf', normed_low, inner_mat, preferred_element_type=...  32.7 us
    pallas_call x1, Pallas kernels, attend(): pl.pallas_call(attend_kernel, grid_spec=pltpu.PrefetchScalarGridSpec(num_...  31.7 us
  transfers between devices with their start and end apart: 4, of which 0 were waited for; matrix products, arithmetic and copies ran while one was open for 11% of the time, Pallas kernels for 23%

profile of v1, /device:TPU:0, one launch (start us, length us, event | category | flops | bytes accessed | tf_op | source)
XLA Modules:
  0.0 1005.4 jit_solution(12860283689142279396)
XLA Ops:
  2.2 2.9 collective-permute-start
  9.6 8.2 concatenate.101
  20.0 139.7 %gather_weights.1 = (bf16[768,384]{1,0:T(8,128)(2,1)}, bf16[768,384]{1,0:T(8,128)(2,1)}, bf16[768,384]{1,0:T(8,128)(2,1)}, bf16[768,384]{1,0:T(8,128)(2,1)}, bf1...) custom-call(bf16[384,384]{1,0:T(8,128)(2,1)} %refs_0_.1, ...), custom_call_target="tpu_custom_call" | custom-call | tf_op jit(solution)/shard_map/gather_weights/pallas_call | solution.py:437
  161.3 2.8 fusion.65
  180.4 44.6 %spread.1 = (bf16[5120,384]{1,0:T(8,128)(2,1)}, bf16[4,512,256]{2,1,0:T(8,128)(2,1)}) custom-call(bf16[4,512,384]{2,1,0:T(8,128)(2,1)} %bitcast.423, bf16[4,512,256]{2,1,0:T(8,128)(2,1)} %bitcast.445), custom_call_target="tpu_custom_call" | custom-call | tf_op jit(solution)/shard_map/spread/pallas_call | solution.py:518
  225.1 2.2 copy-done
  228.5 31.7 %attend.1 = (bf16[2048,256]{1,0:T(8,128)(2,1)S(1)}, f32[256,2048]{1,0:T(8,128)S(1)}, f32[8,2048]{1,0:T(8,128)S(1)}) custom-call(s32[2,8]{1,0:T(2,128)S(1)} %pad_add_fusion.2.bounds, bf16[2048,256]{1,0:T(8,128)(2,1)S(1)} %bitcast.390, bf16[5120,384]{1,0:T(8,128)(2,1)S(1)} %copy-done, f32[8,5120]{1,0:T(8,128)S(1)} %broadcast_in_dim.21.segk_ref, ...), custom_call_target="tpu_custom_call" | custom-call | tf_op jit(solution)/shard_map/attend/pallas_call | solution.py:174
  261.2 14.2 %swap.2 = bf16[4,512,256]{2,1,0:T(8,128)(2,1)} custom-call(bf16[4,512,256]{2,1,0:T(8,128)(2,1)} %bitcast.395), custom_call_target="tpu_custom_call" | custom-call | tf_op jit(solution)/shard_map/swap/pallas_call | solution.py:551
  290.7 3.4 fusion.130
  295.4 2.6 copy.196
  299.1 2.3 copy.197
  312.0 3.5 copy.199
  318.2 15.1 %fusion.38 = bf16[2,512,768]{2,1,0:T(8,128)(2,1)S(1)} fusion(bf16[2,512,768]{2,1,0:T(8,128)(2,1)} %bitcast.398, bf16[2,4,768]{2,1,0:T(4,128)(2,1)} %collective-permute-done.1, bf16[2,4,768]{2,1,0:T(4,128)(2,1)} %collective-permute-done, f32[2,512]{1,0:T(2,128)S(1)} %get-tuple-element.279, f32[768]{0:T(1024)} %reshape.748, ...), kind=kLoop, calls=%fused_computation.75 | loop fusion | flops 47185920 | bytes 3234816 | tf_op jit(solution)/shard_map/convert_element_type | solution.py:910
  339.3 3.2 convolution_add_fusion
  342.5 2.8 copy.152
  345.3 3.7 reshape.705
  349.1 19.6 %add_convert_fusion.4 = bf16[2,512,6,64]{1,0,3,2:T(2,128)(2,1)S(1)} fusion(f32[2,520,6,64]{1,0,3,2:T(2,128)} %reshape.705, f32[2,512,6]{1,0,2:T(2,128)S(1)} %get-tuple-element.266, f32[2,512,6]{1,0,2:T(2,128)S(1)} %get-tuple-element.267, f32[2,512,6]{1,0,2:T(2,128)S(1)} %get-tuple-element.268, f32[2,512,6]{1,0,2:T(2,128)S(1)} %get-tuple-element.269, ...), kind=kLoop, calls=%fused_computation.151 | loop fusion | flops 7077888 | bytes 15163392 | tf_op jit(solution)/shard_map/convert_element_type | solution.py:934
  372.7 32.7 %fusion.11 = (bf16[1024,2,1536]{2,0,1:T(8,128)(2,1)S(1)}, f32[1024,2,1536]{2,0,1:T(8,128)}, f32[2,1536,1024]{1,2,0:T(8,128)}) fusion(f32[2,1536]{1,0:T(2,128)S(1)} %copy-done.177, bf16[2,384,1536]{2,1,0:T(8,128)(2,1)S(1)} %copy-done.208, bf16[1024,2,384]{0,2,1:T(8,128)(2,1)S(1)} %bitcast.460), kind=kOutput, calls=%fused_computation.20 | convolution fusion | flops 2623537152 | bytes 35401728 | tf_op jit(solution)/shard_map/ngd,gdf->ngf/dot_general | solution.py:943
  405.5 3.4 convolution_add_fusion.1
  413.1 2.6 fusion.121
  418.4 16.5 %fusion.147 = (bf16[2,1536]{1,0:T(2,128)(2,1)}, bf16[1024,2,1536]{2,0,1:T(8,128)(2,1)}) fusion(f32[1024,2,1536]{2,0,1:T(8,128)} %get-tuple-element.195, bf16[2,1536,384]{2,1,0:T(8,128)(2,1)} %get-tuple-element.42, bf16[1024,2,384]{0,2,1:T(8,128)(2,1)S(1)} %bitcast.455, f32[2,1536,1024]{1,2,0:T(8,128)} %get-tuple-element.322, f32[2,1536]{1,0:T(2,128)S(1)} %copy-done.177), kind=kOutput, calls=%fused_computation.407 | convolution fusion | flops 2466247680 | bytes 35407872 | tf_op jit(solution)/shard_map/ngd,gfd->ngf/dot_general | solution.py:965
  434.8 5.8 fusion.148
  440.7 2.2 multiply_reduce_fusion.1
  450.3 14.2 %swap.3 = bf16[4,512,256]{2,1,0:T(8,128)(2,1)} custom-call(bf16[4,512,256]{2,1,0:T(8,128)(2,1)} %bitcast.447), custom_call_target="tpu_custom_call" | custom-call | tf_op jit(solution)/shard_map/swap/pallas_call | solution.py:551
  465.8 51.7 %attend_back.1 = (bf16[2048,256]{1,0:T(8,128)(2,1)S(1)}, bf16[5120,384]{1,0:T(8,128)(2,1)}) custom-call(s32[2,8]{1,0:T(2,128)S(1)} %copy-done.11, bf16[2048,256]{1,0:T(8,128)(2,1)S(1)} %bitcast.391, bf16[5120,384]{1,0:T(8,128)(2,1)} %get-tuple-element.49.kv_ref, f32[8,5120]{1,0:T(8,128)S(1)} %copy-done.6, f32[8,2048]{1,0:T(8,128)S(1)} %copy-done.9, ...), custom_call_target="tpu_custom_call" | custom-call | tf_op jit(solution)/shard_map/attend_back/pallas_call | solution.py:267
  517.5 2.1 copy-done.4
  519.6 74.3 %collect.1 = (bf16[4,512,384]{2,1,0:T(8,128)(2,1)S(1)}, bf16[4,512,256]{2,1,0:T(8,128)(2,1)S(1)}) custom-call(bf16[5120,384]{1,0:T(8,128)(2,1)S(1)} %copy-done.4, bf16[4,512,256]{2,1,0:T(8,128)(2,1)S(1)} %bitcast.393), custom_call_target="tpu_custom_call" | custom-call | tf_op jit(solution)/shard_map/collect/pallas_call | solution.py:631
  596.3 3.2 copy.161
  599.4 3.4 reshape.759
  602.9 20.3 %multiply_reduce_fusion.6 = (f32[2,512,6]{1,0,2:T(2,128)S(1)}, f32[2,512,6]{1,0,2:T(2,128)S(1)}, f32[2,512,6]{1,0,2:T(2,128)S(1)}, f32[2,512,6]{1,0,2:T(2,128)S(...) fusion(f32[2,512,6,64]{1,0,3,2:T(2,128)} %reshape.759, ...), kind=kLoop, calls=%fused_computation.142 | loop fusion | flops 10561536 | bytes 30326784 | tf_op jit(solution)/shard_map/reduce_sum | solution.py:991
  631.1 3.4 fusion.119
  635.4 3.9 fusion.53
  640.9 6.3 multiply_multiply_fusion
  647.3 3.7 copy.176
  656.0 2.4 convolution_convert_fusion.3
  658.4 6.8 convolution_convert_fusion.1
  665.2 6.2 convolution_convert_fusion
  673.7 2.7 fusion.149
  678.3 17.5 %pad_add_fusion.1 = f32[2,520,6,64]{1,0,3,2:T(2,128)} fusion(f32[2,512,6,64]{1,0,3,2:T(2,128)S(1)} %copy-done.45, f32[2,512,6,64]{1,0,3,2:T(2,128)S(1)} %copy-done.44, f32[2,512,6,64]{1,0,3,2:T(2,128)S(1)} %copy-done.43, f32[2,512,6,64]{1,0,3,2:T(2,128)S(1)} %copy-done.42, f32[2,512,6,64]{1,0,3,2:T(2,128)S(1)} %copy-done.41, ...), kind=kLoop, calls=%fused_computation.121 | loop fusion | flops 3194880 | bytes 15753216 | tf_op jit(solution)/shard_map/add | solution.py:1000
  695.8 4.7 copy.169
  700.7 12.5 %fusion.45 = (bf16[768]{0:T(1024)(128)(2,1)S(1)}, bf16[768]{0:T(1024)(128)(2,1)S(1)}, bf16[768]{0:T(1024)(128)(2,1)S(1)}, bf16[768]{0:T(1024)(128)(2,1)S(1)}, f3...) fusion(f32[1024,768]{1,0:T(8,128)S(1)} %copy-done.15, ...), kind=kLoop, calls=%fused_computation.82 | loop fusion | flops 25162752 | bytes 17348608 | tf_op jit(solution)/shard_map/reduce_sum | solution.py:1015
  713.2 5.9 pad_add_fusion
  720.8 3.6 collective-permute-start.2
  728.3 1.9 slice_dynamic-update-slice_fusion.9
  730.3 3.1 fusion.67
  743.9 2.3 convert_element_type.559
  746.2 3.1 convert_element_type.560
  749.4 2.0 convert_element_type.562
  751.5 3.1 convert_element_type.563
  754.6 2.6 copy.198
  758.0 2.3 fusion.28
  760.3 2.2 copy-done.25
  767.4 2.1 slice_dynamic-update-slice_fusion.8
  769.6 2.0 slice_dynamic-update-slice_fusion.7
  771.5 2.0 slice_dynamic-update-slice_fusion.6
  780.6 5.6 fusion.24.g_ref
  786.2 171.7 %reduce_grads.1 = bf16[5888,384]{1,0:T(8,128)(2,1)} custom-call(bf16[2,5888,384]{2,1,0:T(8,128)(2,1)} %fusion.24.g_ref), custom_call_target="tpu_custom_call" | custom-call | tf_op jit(solution)/shard_map/reduce_grads/pallas_call | solution.py:769
  958.0 6.5 convert_element_type.565
  974.2 3.9 fusion.150
  978.2 2.7 fusion.151
  985.8 2.5 reshape.735
  989.6 3.7 copy.205
  993.3 8.1 add_add_fusion.2
  1001.4 3.5 copy.206
  (663 shorter events, 149.8 us)
Async XLA Ops:
  0.7 160.6 %copy-start.16 = (bf16[2,1,512,768]{3,2,1,0:T(8,128)(2,1)S(1)}, bf16[2,1,512,768]{3,2,1,0:T(8,128)(2,1)}, u32[]{:S(2)}) copy-start(bf16[2,1,512,768]{3,2,1,0:T(8,128)(2,1)} %param.25) | copy-start | bytes 4718596
  2.2 316.0 %collective-permute-start = (bf16[2,4,768]{2,1,0:T(4,128)(2,1)}, bf16[2,4,768]{2,1,0:T(4,128)(2,1)}, u32[]{:S(2)}, u32[]{:S(2)}) collective-permute-start(bf16[2,4,768]{2,1,0:T(4,128)(2,1)} %get-tuple-element.240), channel_id=1, source_target_pairs={{0,2},{2,4},{4,6},{6,8},{8,10},{10,12},{12,14},{14,16},{16,18},{18... | collective-permute-start | bytes 36872 | tf_op jit(solution)/shard_map/ppermute | solution.py:36
  5.1 313.1 %collective-permute-start.1 = (bf16[2,4,768]{2,1,0:T(4,128)(2,1)}, bf16[2,4,768]{2,1,0:T(4,128)(2,1)}, u32[]{:S(2)}, u32[]{:S(2)}) collective-permute-start(bf16[2,4,768]{2,1,0:T(4,128)(2,1)} %get-tuple-element.241), channel_id=1, source_target_pairs={{2,0},{4,2},{6,4},{8,6},{10,8},{12,10},{14,12},{16,14},{18,16},{20... | collective-permute-start | bytes 36872 | tf_op jit(solution)/shard_map/ppermute | solution.py:39
  8.8 152.4 %copy-start.125 = (s32[1,5120]{1,0:T(1,128)}, s32[1,5120]{1,0:T(1,128)S(1)}, u32[]{:S(2)}) copy-start(s32[1,5120]{1,0:T(1,128)S(1)} %get-tuple-element.197) | copy-start | bytes 61444
  174.9 159.3 %copy-start.35 = (bf16[1024,384]{0,1:T(8,128)(2,1)}, bf16[1024,384]{0,1:T(8,128)(2,1)S(1)}, u32[]{:S(2)}) copy-start(bf16[1024,384]{0,1:T(8,128)(2,1)S(1)} %fusion.66) | copy-start | bytes 2359300
  176.3 48.8 %copy-start.10 = (s32[2,8]{1,0:T(2,128)}, s32[2,8]{1,0:T(2,128)S(1)}, u32[]{:S(2)}) copy-start(s32[2,8]{1,0:T(2,128)S(1)} %pad_add_fusion.2.bounds) | copy-start | bytes 196
  179.2 45.9 %copy-start.146 = (f32[1,5120]{1,0:T(1,128)S(1)}, f32[1,5120]{1,0:T(1,128)}, u32[]{:S(2)}) copy-start(f32[1,5120]{1,0:T(1,128)} %get-tuple-element.196) | copy-start | bytes 61444
  225.1 35.2 %copy-start.5 = (f32[8,5120]{1,0:T(8,128)}, f32[8,5120]{1,0:T(8,128)S(1)}, u32[]{:S(2)}) copy-start(f32[8,5120]{1,0:T(8,128)S(1)} %broadcast_in_dim.21.segk_ref) | copy-start | bytes 491524
  225.1 36.2 %copy-start.8 = (f32[8,2048]{1,0:T(8,128)}, f32[8,2048]{1,0:T(8,128)S(1)}, u32[]{:S(2)}) copy-start(f32[8,2048]{1,0:T(8,128)S(1)} %broadcast_in_dim.23.segq_ref) | copy-start | bytes 196612
  290.6 27.5 %copy-start.122 = (f32[2,512]{1,0:T(2,128)}, f32[2,512]{1,0:T(2,128)S(1)}, u32[]{:S(2)}) copy-start(f32[2,512]{1,0:T(2,128)S(1)} %get-tuple-element.282) | copy-start | bytes 12292
  290.6 46.6 %copy-start.116 = (f32[2,512]{1,0:T(2,128)}, f32[2,512]{1,0:T(2,128)S(1)}, u32[]{:S(2)}) copy-start(f32[2,512]{1,0:T(2,128)S(1)} %get-tuple-element.279) | copy-start | bytes 12292
  290.6 46.6 %copy-start.118 = (f32[2,512]{1,0:T(2,128)}, f32[2,512]{1,0:T(2,128)S(1)}, u32[]{:S(2)}) copy-start(f32[2,512]{1,0:T(2,128)S(1)} %get-tuple-element.280) | copy-start | bytes 12292
  290.6 46.6 %copy-start.120 = (f32[2,512]{1,0:T(2,128)}, f32[2,512]{1,0:T(2,128)S(1)}, u32[]{:S(2)}) copy-start(f32[2,512]{1,0:T(2,128)S(1)} %get-tuple-element.281) | copy-start | bytes 12292
  295.2 12.2 %copy-start.212 = (f32[2,27]{1,0:T(2,128)S(1)}, f32[2,27]{1,0:T(2,128)}, u32[]{:S(2)}) copy-start(f32[2,27]{1,0:T(2,128)} %slice_convert_fusion.22) | copy-start | bytes 652
  295.2 13.7 %copy-start.180 = (f32[2,192]{1,0:T(2,128)S(1)}, f32[2,192]{1,0:T(2,128)}, u32[]{:S(2)}) copy-start(f32[2,192]{1,0:T(2,128)} %get-tuple-element.303) | copy-start | bytes 4612
  295.2 14.4 %copy-start.176 = (f32[2,384]{1,0:T(2,128)S(1)}, f32[2,384]{1,0:T(2,128)}, u32[]{:S(2)}) copy-start(f32[2,384]{1,0:T(2,128)} %get-tuple-element.301) | copy-start | bytes 9220
  295.2 15.0 %copy-start.175 = (f32[2,384]{1,0:T(2,128)S(1)}, f32[2,384]{1,0:T(2,128)}, u32[]{:S(2)}) copy-start(f32[2,384]{1,0:T(2,128)} %get-tuple-element.300) | copy-start | bytes 9220
  295.2 15.6 %copy-start.174 = (f32[2,384]{1,0:T(2,128)S(1)}, f32[2,384]{1,0:T(2,128)}, u32[]{:S(2)}) copy-start(f32[2,384]{1,0:T(2,128)} %get-tuple-element.299) | copy-start | bytes 9220
  295.3 16.1 %copy-start.173 = (f32[2,384]{1,0:T(2,128)S(1)}, f32[2,384]{1,0:T(2,128)}, u32[]{:S(2)}) copy-start(f32[2,384]{1,0:T(2,128)} %get-tuple-element.296) | copy-start | bytes 9220
  315.5 17.8 %copy-start.101 = (bf16[768,384]{1,0:T(8,128)(2,1)S(1)}, bf16[768,384]{1,0:T(8,128)(2,1)}, u32[]{:S(2)}) copy-start(bf16[768,384]{1,0:T(8,128)(2,1)} %get-tuple-element.51) | copy-start | bytes 1769476
  316.8 16.4 %copy-start.199 = (f32[384]{0:T(512)S(1)}, f32[384]{0:T(512)}, u32[]{:S(2)}) copy-start(f32[384]{0:T(512)} %reshape.749) | copy-start | bytes 4612
  318.2 17.4 %copy-start.105 = (bf16[384,54]{0,1:T(8,128)(2,1)S(1)}, bf16[384,54]{0,1:T(8,128)(2,1)}, u32[]{:S(2)}) copy-start(bf16[384,54]{0,1:T(8,128)(2,1)} %reshape.702) | copy-start | bytes 124420
  318.2 17.4 %copy-start.206 = (f32[54]{0:T(128)S(1)}, f32[54]{0:T(128)}, u32[]{:S(2)}) copy-start(f32[54]{0:T(128)} %reshape.750) | copy-start | bytes 652
  337.4 11.6 %copy-start.107 = (f32[2,512,6]{1,0,2:T(2,128)}, f32[2,512,6]{1,0,2:T(2,128)S(1)}, u32[]{:S(2)}) copy-start(f32[2,512,6]{1,0,2:T(2,128)S(1)} %get-tuple-element.265) | copy-start | bytes 73732
  337.4 11.6 %copy-start.108 = (f32[2,512,6]{1,0,2:T(2,128)}, f32[2,512,6]{1,0,2:T(2,128)S(1)}, u32[]{:S(2)}) copy-start(f32[2,512,6]{1,0,2:T(2,128)S(1)} %get-tuple-element.266) | copy-start | bytes 73732
  337.4 11.6 %copy-start.109 = (f32[2,512,6]{1,0,2:T(2,128)}, f32[2,512,6]{1,0,2:T(2,128)S(1)}, u32[]{:S(2)}) copy-start(f32[2,512,6]{1,0,2:T(2,128)S(1)} %get-tuple-element.267) | copy-start | bytes 73732
  337.4 11.6 %copy-start.110 = (f32[2,512,6]{1,0,2:T(2,128)}, f32[2,512,6]{1,0,2:T(2,128)S(1)}, u32[]{:S(2)}) copy-start(f32[2,512,6]{1,0,2:T(2,128)S(1)} %get-tuple-element.268) | copy-start | bytes 73732
  337.4 11.6 %copy-start.111 = (f32[2,512,6]{1,0,2:T(2,128)}, f32[2,512,6]{1,0,2:T(2,128)S(1)}, u32[]{:S(2)}) copy-start(f32[2,512,6]{1,0,2:T(2,128)S(1)} %get-tuple-element.269) | copy-start | bytes 73732
  337.4 11.6 %copy-start.112 = (f32[2,512,6]{1,0,2:T(2,128)}, f32[2,512,6]{1,0,2:T(2,128)S(1)}, u32[]{:S(2)}) copy-start(f32[2,512,6]{1,0,2:T(2,128)S(1)} %get-tuple-element.270) | copy-start | bytes 73732
  349.1 19.8 %copy-start.46 = (bf16[1024,768]{0,1:T(8,128)(2,1)S(1)}, bf16[1024,768]{0,1:T(8,128)(2,1)}, u32[]{:S(2)}) copy-start(bf16[1024,768]{0,1:T(8,128)(2,1)} %copy.196) | copy-start | bytes 4718596
  349.1 19.8 %copy-start.90 = (bf16[1024,384]{0,1:T(8,128)(2,1)S(1)}, bf16[1024,384]{0,1:T(8,128)(2,1)}, u32[]{:S(2)}) copy-start(bf16[1024,384]{0,1:T(8,128)(2,1)} %copy.197) | copy-start | bytes 2359300
  349.1 19.8 %copy-start.188 = (f32[768]{0:T(1024)S(1)}, f32[768]{0:T(1024)}, u32[]{:S(2)}) copy-start(f32[768]{0:T(1024)} %reshape.752) | copy-start | bytes 9220
  349.1 19.8 %copy-start.210 = (bf16[768,768]{1,0:T(8,128)(2,1)S(1)}, bf16[768,768]{1,0:T(8,128)(2,1)}, u32[]{:S(2)}) copy-start(bf16[768,768]{1,0:T(8,128)(2,1)} %get-tuple-element.53) | copy-start | bytes 3538948
  371.0 34.4 %copy-start.156 = (f32[1024]{0:T(1024)}, f32[1024]{0:T(1024)S(1)}, u32[]{:S(2)}) copy-start(f32[1024]{0:T(1024)S(1)} %multiply_reduce_fusion.5) | copy-start | bytes 12292
  371.8 33.7 %copy-start.80 = (bf16[1024,768]{0,1:T(8,128)(2,1)}, bf16[1024,768]{0,1:T(8,128)(2,1)S(1)}, u32[]{:S(2)}) copy-start(bf16[1024,768]{0,1:T(8,128)(2,1)S(1)} %fusion.55) | copy-start | bytes 4718596
  372.7 32.8 %copy-start.197 = (f32[2,384]{1,0:T(2,128)S(1)}, f32[2,384]{1,0:T(2,128)}, u32[]{:S(2)}) copy-start(f32[2,384]{1,0:T(2,128)} %get-tuple-element.298) | copy-start | bytes 9220
  372.7 32.8 %copy-start.209 = (bf16[2,1536,384]{2,1,0:T(8,128)(2,1)S(1)}, bf16[2,1536,384]{2,1,0:T(8,128)(2,1)}, u32[]{:S(2)}) copy-start(bf16[2,1536,384]{2,1,0:T(8,128)(2,1)} %get-tuple-element.42) | copy-start | bytes 7077892
  418.4 16.5 %copy-start.74 = (bf16[1024,768]{0,1:T(8,128)(2,1)}, bf16[1024,768]{0,1:T(8,128)(2,1)S(1)}, u32[]{:S(2)}) copy-start(bf16[1024,768]{0,1:T(8,128)(2,1)S(1)} %get-tuple-element.176) | copy-start | bytes 4718596
  449.0 15.5 %copy-start.3 = (bf16[4,512,256]{2,1,0:T(8,128)(2,1)S(1)}, bf16[4,512,256]{2,1,0:T(8,128)(2,1)}, u32[]{:S(2)}) copy-start(bf16[4,512,256]{2,1,0:T(8,128)(2,1)} %get-tuple-element.48) | copy-start | bytes 3145732
  449.0 15.5 %copy-start.6 = (f32[8,5120]{1,0:T(8,128)S(1)}, f32[8,5120]{1,0:T(8,128)}, u32[]{:S(2)}) copy-start(f32[8,5120]{1,0:T(8,128)} %copy-done.5) | copy-start | bytes 491524
  449.0 15.5 %copy-start.9 = (f32[8,2048]{1,0:T(8,128)S(1)}, f32[8,2048]{1,0:T(8,128)}, u32[]{:S(2)}) copy-start(f32[8,2048]{1,0:T(8,128)} %copy-done.8) | copy-start | bytes 196612
  449.0 15.5 %copy-start.11 = (s32[2,8]{1,0:T(2,128)S(1)}, s32[2,8]{1,0:T(2,128)}, u32[]{:S(2)}) copy-start(s32[2,8]{1,0:T(2,128)} %copy-done.10) | copy-start | bytes 196
  602.8 20.4 %copy-start.142 = (f32[2,512]{1,0:T(2,128)S(1)}, f32[2,512]{1,0:T(2,128)}, u32[]{:S(2)}) copy-start(f32[2,512]{1,0:T(2,128)} %get-tuple-element.287) | copy-start | bytes 12292
  602.8 20.5 %copy-start.139 = (f32[2,512]{1,0:T(2,128)S(1)}, f32[2,512]{1,0:T(2,128)}, u32[]{:S(2)}) copy-start(f32[2,512]{1,0:T(2,128)} %get-tuple-element.286) | copy-start | bytes 12292
  602.8 20.5 %copy-start.136 = (f32[2,512]{1,0:T(2,128)S(1)}, f32[2,512]{1,0:T(2,128)}, u32[]{:S(2)}) copy-start(f32[2,512]{1,0:T(2,128)} %get-tuple-element.285) | copy-start | bytes 12292
  602.8 20.5 %copy-start.133 = (f32[2,512]{1,0:T(2,128)S(1)}, f32[2,512]{1,0:T(2,128)}, u32[]{:S(2)}) copy-start(f32[2,512]{1,0:T(2,128)} %get-tuple-element.284) | copy-start | bytes 12292
  602.9 20.5 %copy-start.130 = (f32[2,512]{1,0:T(2,128)S(1)}, f32[2,512]{1,0:T(2,128)}, u32[]{:S(2)}) copy-start(f32[2,512]{1,0:T(2,128)} %get-tuple-element.283) | copy-start | bytes 12292
  602.9 20.6 %copy-start.124 = (f32[2,512]{1,0:T(2,128)S(1)}, f32[2,512]{1,0:T(2,128)}, u32[]{:S(2)}) copy-start(f32[2,512]{1,0:T(2,128)} %copy-done.122) | copy-start | bytes 12292
  602.9 20.6 %copy-start.121 = (f32[2,512]{1,0:T(2,128)S(1)}, f32[2,512]{1,0:T(2,128)}, u32[]{:S(2)}) copy-start(f32[2,512]{1,0:T(2,128)} %copy-done.120) | copy-start | bytes 12292
  602.9 20.6 %copy-start.119 = (f32[2,512]{1,0:T(2,128)S(1)}, f32[2,512]{1,0:T(2,128)}, u32[]{:S(2)}) copy-start(f32[2,512]{1,0:T(2,128)} %copy-done.118) | copy-start | bytes 12292
  602.9 20.6 %copy-start.117 = (f32[2,512]{1,0:T(2,128)S(1)}, f32[2,512]{1,0:T(2,128)}, u32[]{:S(2)}) copy-start(f32[2,512]{1,0:T(2,128)} %copy-done.116) | copy-start | bytes 12292
  602.9 20.7 %copy-start.52 = (f32[2,512,6,9]{1,0,3,2:T(2,128)S(1)}, f32[2,512,6,9]{1,0,3,2:T(2,128)}, u32[]{:S(2)}) copy-start(f32[2,512,6,9]{1,0,3,2:T(2,128)} %copy-done.51) | copy-start | bytes 663556
  602.9 20.7 %copy-start.95 = (f32[2,512,6]{1,0,2:T(2,128)S(1)}, f32[2,512,6]{1,0,2:T(2,128)}, u32[]{:S(2)}) copy-start(f32[2,512,6]{1,0,2:T(2,128)} %copy-done.94) | copy-start | bytes 73732
  602.9 20.7 %copy-start.144 = (f32[2,512,6]{1,0,2:T(2,128)S(1)}, f32[2,512,6]{1,0,2:T(2,128)}, u32[]{:S(2)}) copy-start(f32[2,512,6]{1,0,2:T(2,128)} %multiply_divide_fusion) | copy-start | bytes 73732
  602.9 20.9 %copy-start.104 = (f32[2,512,6]{1,0,2:T(2,128)S(1)}, f32[2,512,6]{1,0,2:T(2,128)}, u32[]{:S(2)}) copy-start(f32[2,512,6]{1,0,2:T(2,128)} %copy-done.103) | copy-start | bytes 73732
  651.2 20.3 %copy-start.59 = (bf16[2,512,384]{2,1,0:T(8,128)(2,1)}, bf16[2,512,384]{2,1,0:T(8,128)(2,1)S(1)}, u32[]{:S(2)}) copy-start(bf16[2,512,384]{2,1,0:T(8,128)(2,1)S(1)} %get-tuple-element.227) | copy-start | bytes 2359300
  700.6 12.6 %copy-start.30 = (f32[2,512,768]{2,1,0:T(8,128)S(1)}, f32[2,512,768]{2,1,0:T(8,128)}, u32[]{:S(2)}) copy-start(f32[2,512,768]{2,1,0:T(8,128)} %get-tuple-element.212) | copy-start | bytes 9437188
  700.6 12.6 %copy-start.31 = (f32[2,512,768]{2,1,0:T(8,128)S(1)}, f32[2,512,768]{2,1,0:T(8,128)}, u32[]{:S(2)}) copy-start(f32[2,512,768]{2,1,0:T(8,128)} %get-tuple-element.213) | copy-start | bytes 9437188
  700.6 12.6 %copy-start.32 = (f32[2,512,768]{2,1,0:T(8,128)S(1)}, f32[2,512,768]{2,1,0:T(8,128)}, u32[]{:S(2)}) copy-start(f32[2,512,768]{2,1,0:T(8,128)} %get-tuple-element.214) | copy-start | bytes 9437188
  700.7 12.6 %copy-start.33 = (f32[2,512,768]{2,1,0:T(8,128)S(1)}, f32[2,512,768]{2,1,0:T(8,128)}, u32[]{:S(2)}) copy-start(f32[2,512,768]{2,1,0:T(8,128)} %get-tuple-element.215) | copy-start | bytes 9437188
  700.7 12.6 %copy-start.34 = (f32[2,512,768]{2,1,0:T(8,128)S(1)}, f32[2,512,768]{2,1,0:T(8,128)}, u32[]{:S(2)}) copy-start(f32[2,512,768]{2,1,0:T(8,128)} %get-tuple-element.216) | copy-start | bytes 9437188
  720.8 36.3 %collective-permute-start.2 = (bf16[2,4,1152]{2,1,0:T(4,128)(2,1)S(1)}, bf16[2,4,1152]{2,1,0:T(4,128)(2,1)}, u32[]{:S(2)}, u32[]{:S(2)}) collective-permute-start(bf16[2,4,1152]{2,1,0:T(4,128)(2,1)S(1)} %get-tuple-element.217), channel_id=1, source_target_pairs={{0,2},{2,4},{4,6},{6,8},{8,10},{10,12},{12,14},{14,16},{16,18},{18... | collective-permute-start | bytes 55304 | tf_op jit(solution)/shard_map/ppermute | solution.py:36
  724.5 32.7 %collective-permute-start.3 = (bf16[2,4,1152]{2,1,0:T(4,128)(2,1)S(1)}, bf16[2,4,1152]{2,1,0:T(4,128)(2,1)}, u32[]{:S(2)}, u32[]{:S(2)}) collective-permute-start(bf16[2,4,1152]{2,1,0:T(4,128)(2,1)S(1)} %get-tuple-element.218), channel_id=1, source_target_pairs={{2,0},{4,2},{6,4},{8,6},{10,8},{12,10},{14,12},{16,14},{18,16},{20... | collective-permute-start | bytes 55304 | tf_op jit(solution)/shard_map/ppermute | solution.py:39
  967.8 13.1 %slice-start = ((s8[4718592]{0:T(1024)(128)(4,1)}), s8[524288]{0:T(1024)(128)(4,1)S(1)}, s32[]{:S(2)}) async-start(s8[4718592]{0:T(1024)(128)(4,1)} %bitcast.409), calls=%async_computation | async-start | bytes 1048576
  (158 other events, 620.9 us)
